TPU v7x, 32 devices: a whole 2x2x4 slice. The times are simulated.
32 devices in a mesh: gx: 4 (over y, x), gy: 4 (over z), gz: 2 (over core).
Axes of the slice: x: 2, y: 2, z: 4, core: 2. Of those that a mesh axis runs over, the one named last changes fastest.
Arguments:
- populations: float32 [19, 16, 64, 256], P(None, 'gx', 'gy', 'gz'), may hold values from 0.02 to 0.12
- solid: int32 [16, 64, 256], P('gx', 'gy', 'gz'), may hold values 0 or 1
- coefficients: float32 [512, 16, 256], P(('gx', 'gz')), may hold values from -0.09375 to 0.09375
- body_nodes: float32 [3, 512, 512], P(None, 'gy', ('gx', 'gz')), may hold values from -2 to 2
- centers: float32 [3, 512], P(None, ('gx', 'gz')), may hold values from -0.5 to 0.5
- angles: float32 [3, 512], P(None, ('gx', 'gz')), may hold values from -3.140625 to 3.140625
- velocity: float32 [6, 512], P(None, ('gx', 'gz')), may hold values from -0.5 to 0.5
- node_frac: float32 [3, 512, 512], P(None, 'gy', ('gx', 'gz')), may hold values from 0 to 1
- node_cell: int32 [512, 512], P('gy', ('gx', 'gz')), may hold values from 0 to 6014, as said below
- grain_tile: int32 [4, 512, 1], P('gy', ('gx', 'gz')), may hold values from 0 to 7; in each aligned block of 64 rows (0 to 63, 64 to 127, ..., all dimensions but the last counted through in order) at most 16 rows name the same one
- send_grain: int32 [8, 32], P(('gx', 'gz')), may hold values from -1 to 63, as said below
- recv_partner: int32 [8, 32], P(('gx', 'gz')), may hold values from -1 to 63, as said below
Outputs:
- populations_out: float32 [19, 16, 64, 256], P(None, 'gx', 'gy', 'gz')
- centers_out: float32 [3, 512], P(None, ('gx', 'gz'))
- velocity_out: float32 [6, 512], P(None, ('gx', 'gz'))
Inputs may be any that keep to these rules, and one draw needn't show every extreme that they name: `node_cell`: c = (x * 16 + y) * 128 + z with x < 3, y < 15, z < 127, so all eight corners lie in the tile. `grain_tile`: in the rows of one device at most 16 grains name the same tile, a bound that some block reaches. `send_grain`: -1 marks an empty slot; within each destination's 4 slots the live ones come first; slot k for destination d on source s is live exactly when slot k for source s on owner d is live in recv_partner; some owner receives all 4 slots live from every source. `recv_partner`: -1 marks an empty slot, matching send_grain as stated there.
All inputs are finite; a program needn't handle non-finite values. No bound on the sum of `solid` on one device may be relied on, other than what follows from the above.
Results may differ from a plain program's by a relative error of at most 0.0001.
Values sent between devices are 32-bit elements; how exact they have to be, the bound alone decides.
A program may use at most 128 MiB of HBM per device.

v0:
```python
import functools
import math

import jax
import jax.numpy as jnp
import numpy as np
from jax import lax
from jax.experimental import pallas as pl
from jax.experimental.pallas import tpu as pltpu
from jax.sharding import PartitionSpec as P

STEPS = 2

highest = lax.Precision.HIGHEST
lattice_dirs = np.array(
    [
        [0, 0, 0],
        [1, 0, 0],
        [-1, 0, 0],
        [0, 1, 0],
        [0, -1, 0],
        [0, 0, 1],
        [0, 0, -1],
        [1, 1, 0],
        [-1, -1, 0],
        [1, -1, 0],
        [-1, 1, 0],
        [1, 0, 1],
        [-1, 0, -1],
        [1, 0, -1],
        [-1, 0, 1],
        [0, 1, 1],
        [0, -1, -1],
        [0, 1, -1],
        [0, -1, 1],
    ],
    dtype=np.int32,
)
lattice_weights = [1.0 / 3.0] + [1.0 / 18.0] * 6 + [1.0 / 36.0] * 12
opposite_dirs = np.array(
    [0, 2, 1, 4, 3, 6, 5, 8, 7, 10, 9, 12, 11, 14, 13, 16, 15, 18, 17], dtype=np.int32
)
tau_relax = 0.9
ib_stiffness = 0.5
contact_stiffness = 0.05
time_step = 0.05
bf16 = jnp.bfloat16
f32 = jnp.float32


def padded_2(cells, sides, width):
    for axis, dim in sides:
        count = lax.axis_size(axis)
        head = lax.slice_in_dim(cells, 0, width, axis=dim)
        tail = lax.slice_in_dim(cells, cells.shape[dim] - width, cells.shape[dim], axis=dim)
        cells = jnp.concatenate(
            [
                lax.ppermute(tail, axis, [(i, (i + 1) % count) for i in range(count)]),
                cells,
                lax.ppermute(head, axis, [((i + 1) % count, i) for i in range(count)]),
            ],
            axis=dim,
        )
    return cells


def stream(post, solid):
    directions = post.shape[0]
    moved = post
    for axis_part, axis in enumerate(("gx", "gy", "gz")):
        chosen = [d for d in range(directions) if lattice_dirs[d][axis_part] != 0]
        selected = moved[np.array(chosen, dtype=np.int32)]
        padded = padded_2(selected, ((axis, axis_part + 1),), 1)
        extent = selected.shape[axis_part + 1]
        shifted = [
            lax.slice_in_dim(
                padded[position],
                1 - int(lattice_dirs[direction][axis_part]),
                1 - int(lattice_dirs[direction][axis_part]) + extent,
                axis=axis_part,
            )
            for position, direction in enumerate(chosen)
        ]
        moved = moved.at[np.array(chosen, dtype=np.int32)].set(jnp.stack(shifted))
    return jnp.where(solid[None] > 0, moved[opposite_dirs], moved)


def rotation_rows(angles):
    ca, sa = jnp.cos(angles[0]), jnp.sin(angles[0])
    cb, sb = jnp.cos(angles[1]), jnp.sin(angles[1])
    cc, sc = jnp.cos(angles[2]), jnp.sin(angles[2])
    return [
        cc * cb,
        cc * sb * sa - sc * ca,
        cc * sb * ca + sc * sa,
        sc * cb,
        sc * sb * sa + cc * ca,
        sc * sb * ca - cc * sa,
        -sb,
        cb * sa,
        cb * ca,
    ]


def advance_rows(rows, totals):
    rotation, centre, motion = rows[0:9], rows[9:12], rows[12:18]
    motion = [motion[i] + time_step * totals[i] for i in range(6)]
    centre = [centre[i] + time_step * motion[i] for i in range(3)]
    spin = motion[3:6]
    turned = []
    for i in range(3):
        j, k = (i + 1) % 3, (i + 2) % 3
        for c in range(3):
            cross = spin[j] * rotation[3 * k + c] - spin[k] * rotation[3 * j + c]
            turned.append(rotation[3 * i + c] + time_step * cross)
    return turned + centre + motion


def cross(left, right):
    return [
        left[1] * right[2] - left[2] * right[1],
        left[2] * right[0] - left[0] * right[2],
        left[0] * right[1] - left[1] * right[0],
    ]


def split(values):
    high = values.astype(bf16)
    return high, (values - high.astype(f32)).astype(bf16)


def pack_kernel(index_ref, name_ref, tiles_ref, out_ref):
    row = lax.broadcasted_iota(jnp.int32, tiles_ref.shape[1:], 0)

    def body(slot, carry):
        tile = tiles_ref[index_ref[slot]]
        out_ref[slot] = jnp.where(row == 7, name_ref[slot], tile)
        return carry

    lax.fori_loop(0, out_ref.shape[0], body, 0, unroll=8)


def pack(index, name, tiles):
    return pl.pallas_call(
        pack_kernel,
        out_shape=jax.ShapeDtypeStruct((index.shape[0],) + tiles.shape[1:], f32),
        in_specs=[
            pl.BlockSpec(memory_space=pltpu.SMEM),
            pl.BlockSpec(memory_space=pltpu.SMEM),
            pl.BlockSpec(memory_space=pltpu.VMEM),
        ],
        out_specs=pl.BlockSpec(memory_space=pltpu.VMEM),
    )(index, name, tiles)


def columns(matrix, count):
    return [matrix[:, i : i + 1] for i in range(count)]


def lane_pack(values):
    rows = values[0].shape[0]
    lane = lax.broadcasted_iota(jnp.int32, (rows, 128), 1)
    out = jnp.zeros((rows, 128), f32)
    for i, value in enumerate(values):
        out = jnp.where(lane == i, value, out)
    return out


def total(values):
    return jnp.sum(values, axis=1, keepdims=True)


def step_kernel(
    size_y,
    tile_cap,
    chunk,
    counts_ref,
    pick_ref,
    state_ref,
    slots_ref,
    contacts_ref,
    holder_ref,
    coef_ref,
    fluid_ref,
    solid_ref,
    post_ref,
    loads_ref,
    poly_ref,
    level_ref,
    grid_ref,
    speed_ref,
    force_ref,
    cell_ref,
    velocity_ref,
):
    state = state_ref[...]
    grains = state.shape[1]
    tile_slots, _, nodes = slots_ref.shape
    contact_slots = contacts_ref.shape[0]
    order = coef_ref.shape[1]
    directions, plane, size_z = fluid_ref.shape
    size_x = plane // size_y

    def one_hot(ids):
        lane = lax.broadcasted_iota(jnp.int32, (ids.shape[0], grains), 1).astype(f32)
        return jnp.where(lane == ids, 1.0, 0.0)

    def picked(hot):
        found = lax.dot_general(
            hot, state, (((1,), (1,)), ((), ())), precision=highest, preferred_element_type=f32
        )
        return columns(found, 18)

    def gathered(values, hot):
        return lax.dot_general(
            lane_pack(values), hot, (((0,), (0,)), ((), ())), precision=highest, preferred_element_type=f32
        )[0:8]

    partner_hot = one_hot(contacts_ref[:, 7, :][:, 0:1])
    holder_hot = one_hot(holder_ref[...])
    partner = picked(partner_hot)
    holder = picked(holder_hot)
    alive = jnp.where(holder_ref[...] >= 0.0, 1.0, 0.0)
    body = [contacts_ref[:, i, :] for i in range(3)]
    arm = [
        partner[3 * i] * body[0] + partner[3 * i + 1] * body[1] + partner[3 * i + 2] * body[2]
        for i in range(3)
    ]
    rel = [(partner[9 + i] + arm[i]) - holder[9 + i] for i in range(3)]
    for d in range(3):
        y = jnp.clip(holder[d] * rel[0] + holder[3 + d] * rel[1] + holder[6 + d] * rel[2], -1.0, 1.0)
        first = [jnp.ones_like(y), y]
        second = [jnp.ones_like(y), 2.0 * y]
        for degree in range(2, order):
            first.append(2.0 * y * first[-1] - first[-2])
            second.append(2.0 * y * second[-1] - second[-2])
        for degree in range(order):
            slope = degree * second[degree - 1] if degree else jnp.zeros_like(y)
            poly_ref[2 * d, :, degree, :] = first[degree]
            poly_ref[2 * d + 1, :, degree, :] = slope

    def contact(slot, carry):
        high, low = split(coef_ref[pick_ref[slot]])
        table = jnp.concatenate([high, low, high], axis=0)
        along = jnp.concatenate([poly_ref[0, slot], poly_ref[1, slot]], axis=1)
        along_high, along_low = split(along)
        along = jnp.concatenate([along_high, along_high, along_low], axis=0)
        part = lax.dot_general(table, along, (((0,), (0,)), ((), ())), preferred_element_type=f32)
        poly_y, slope_y = poly_ref[2, slot], poly_ref[3, slot]
        poly_z, slope_z = poly_ref[4, slot], poly_ref[5, slot]
        value = slope_xp = slope_yp = None
        for b in range(order):
            here = part[b * order : (b + 1) * order, 0:nodes]
            there = part[b * order : (b + 1) * order, nodes : 2 * nodes]
            t, s = poly_y[b : b + 1], slope_y[b : b + 1]
            if b == 0:
                value, slope_xp, slope_yp = here * t, there * t, here * s
            else:
                value, slope_xp, slope_yp = value + here * t, slope_xp + there * t, slope_yp + here * s
        for i, terms in enumerate((value * poly_z, slope_xp * poly_z, slope_yp * poly_z, value * slope_z)):
            level_ref[i, pl.ds(slot, 1), :] = jnp.sum(terms, axis=0, keepdims=True)
        return carry

    lax.fori_loop(0, contact_slots, contact, 0, unroll=math.gcd(contact_slots, 4))

    gradient = [level_ref[i + 1] for i in range(3)]
    depth = jnp.maximum(-level_ref[0], 0.0)
    norm = gradient[0] * gradient[0] + gradient[1] * gradient[1] + gradient[2] * gradient[2]
    strength = contact_stiffness * depth / jnp.sqrt(1.0 + norm) * alive
    push = [
        (holder[3 * i] * gradient[0] + holder[3 * i + 1] * gradient[1] + holder[3 * i + 2] * gradient[2])
        * strength
        for i in range(3)
    ]
    sums = [total(push[i]) for i in range(3)]
    on_holder = [-s for s in sums] + [-total(t) for t in cross(rel, push)]
    on_partner = sums + [total(t) for t in cross(arm, push)]
    loads = gathered(on_holder, holder_hot) + gathered(on_partner, partner_hot)

    density = fluid_ref[0]
    momentum = [None, None, None]
    for q in range(1, directions):
        values = fluid_ref[q]
        density = density + values
        for i in range(3):
            e = int(lattice_dirs[q][i])
            if e:
                term = values if e > 0 else -values
                momentum[i] = term if momentum[i] is None else momentum[i] + term
    inverse = 1.0 / density
    for i in range(3):
        flow = momentum[i] * inverse
        velocity_ref[i] = flow
        high, low = split(flow)
        rows = pl.ds(i * plane, plane)
        grid_ref[rows, 0:size_z] = high
        grid_ref[rows, size_z : 2 * size_z] = low
        grid_ref[rows, 2 * size_z : 3 * size_z] = high

    slot_hot = one_hot(slots_ref[:, 7, :][:, 0:1])
    own = picked(slot_hot)
    body = [slots_ref[:, i, :] for i in range(3)]
    arm = [own[3 * i] * body[0] + own[3 * i + 1] * body[1] + own[3 * i + 2] * body[2] for i in range(3)]
    swirl = cross(own[15:18], arm)
    for i in range(3):
        speed_ref[:, i, :] = own[12 + i] + swirl[i]
    force_ref[...] = jnp.zeros_like(force_ref)
    cell_ref[...] = jnp.zeros_like(cell_ref)
    depth_row = lax.broadcasted_iota(jnp.int32, (size_z, nodes), 0).astype(f32)
    y_row = lax.broadcasted_iota(jnp.int32, (size_y, nodes), 0).astype(f32)

    def spread(start):
        highs, lows, plane_weights = [], [], []
        for k in range(chunk):
            tile = slots_ref[start + k]
            cell = tile[6:7]
            line = jnp.floor((cell + 0.5) * (1.0 / size_z))
            base_z = cell - line * size_z
            base_x = jnp.floor((line + 0.5) * (1.0 / size_y))
            base_y = line - base_x * size_y
            upper, lower = tile[5:6], 1.0 - tile[5:6]
            upper_high = upper.astype(bf16).astype(f32)
            lower_high = lower.astype(bf16).astype(f32)
            at_low, at_high = depth_row == base_z, depth_row == base_z + 1.0
            highs.append(
                jnp.where(at_low, lower_high, jnp.where(at_high, upper_high, 0.0)).astype(bf16)
            )
            lows.append(
                jnp.where(
                    at_low, lower - lower_high, jnp.where(at_high, upper - upper_high, 0.0)
                ).astype(bf16)
            )
            frac_y = tile[4:5]
            weight_y = jnp.where(
                y_row == base_y, 1.0 - frac_y, jnp.where(y_row == base_y + 1.0, frac_y, 0.0)
            )
            frac_x = tile[3:4]
            rows = []
            for x in range(size_x):
                weight_x = jnp.where(
                    base_x == float(x), 1.0 - frac_x, jnp.where(base_x == float(x - 1), frac_x, 0.0)
                )
                rows.append(weight_x * weight_y)
            plane_weights.append(jnp.concatenate(rows, axis=0))
        high = jnp.concatenate(highs, axis=1)
        low = jnp.concatenate(lows, axis=1)
        lines = jnp.dot(
            grid_ref[...], jnp.concatenate([high, high, low], axis=0), preferred_element_type=f32
        )
        spread_high, spread_low = [], []
        for k in range(chunk):
            weights = plane_weights[k]
            live = jnp.where(slots_ref[start + k][7:8] >= 0.0, ib_stiffness, 0.0)
            speed = speed_ref[start + k]
            pieces, forces = [], []
            for i in range(3):
                taken = lines[i * plane : (i + 1) * plane, k * nodes : (k + 1) * nodes]
                interp = jnp.sum(taken * weights, axis=0, keepdims=True)
                node = live * (speed[i : i + 1] - interp)
                force_ref[start + k, i : i + 1, :] = node
                pieces.append(node * weights)
            piece_high, piece_low = split(jnp.concatenate(pieces, axis=0))
            spread_high.append(piece_high)
            spread_low.append(piece_low)
        contract = (((1,), (1,)), ((), ()))
        wide = lax.dot_general(
            jnp.concatenate(spread_high, axis=1),
            jnp.concatenate([high, low], axis=0),
            contract,
            preferred_element_type=f32,
        )
        narrow = lax.dot_general(
            jnp.concatenate(spread_low, axis=1), high, contract, preferred_element_type=f32
        )
        cell_ref[...] += wide[:, 0:size_z] + wide[:, size_z : 2 * size_z] + narrow

    for source in range(tile_slots // tile_cap):

        def body_of(turn, carry, source=source):
            spread(source * tile_cap + turn * chunk)
            return carry

        lax.fori_loop(0, (counts_ref[source] + chunk - 1) // chunk, body_of, 0)

    node = [force_ref[:, i, :] for i in range(3)]
    back = [-total(node[i]) for i in range(3)] + [-total(t) for t in cross(arm, node)]
    loads_ref[...] = loads + gathered(back, slot_hot)

    for x in range(size_x):
        rows = slice(x * size_y, (x + 1) * size_y)
        density = fluid_ref[0, rows]
        for q in range(1, directions):
            density = density + fluid_ref[q, rows]
        scale = tau_relax / density
        shifted = [
            velocity_ref[i, rows] + scale * cell_ref[i * plane + x * size_y : i * plane + (x + 1) * size_y, :]
            for i in range(3)
        ]
        speed = shifted[0] * shifted[0] + shifted[1] * shifted[1] + shifted[2] * shifted[2]
        base = 1.0 - 1.5 * speed
        wall = solid_ref[rows] > 0
        for q in range(directions):
            flat = fluid_ref[q, rows]
            along = None
            for i in range(3):
                e = int(lattice_dirs[q][i])
                if e:
                    term = shifted[i] if e > 0 else -shifted[i]
                    along = term if along is None else along + term
            inside = base if along is None else base + along * (3.0 + 4.5 * along)
            balance = lattice_weights[q] * density * inside
            relaxed = flat - (flat - balance) * (1.0 / tau_relax)
            post_ref[q, rows] = jnp.where(wall, flat, relaxed)


def run_step(size_y, tile_cap, counts, pick, state, slots, contacts, holder, coefs, fluid, solid):
    grains = state.shape[1]
    tile_slots, _, nodes = slots.shape
    contact_slots = contacts.shape[0]
    order = coefs.shape[1]
    directions, plane, size_z = fluid.shape
    vmem = pl.BlockSpec(memory_space=pltpu.VMEM)
    smem = pl.BlockSpec(memory_space=pltpu.SMEM)
    return pl.pallas_call(
        functools.partial(step_kernel, size_y, tile_cap, math.gcd(tile_cap, 4)),
        out_shape=(
            jax.ShapeDtypeStruct(fluid.shape, f32),
            jax.ShapeDtypeStruct((8, grains), f32),
        ),
        in_specs=[smem, smem] + [vmem] * 7,
        out_specs=(vmem, vmem),
        scratch_shapes=[
            pltpu.VMEM((6, contact_slots, order, nodes), f32),
            pltpu.VMEM((4, contact_slots, nodes), f32),
            pltpu.VMEM((3 * plane, 3 * size_z), bf16),
            pltpu.VMEM((tile_slots, 8, nodes), f32),
            pltpu.VMEM((tile_slots, 8, nodes), f32),
            pltpu.VMEM((3 * plane, size_z), f32),
            pltpu.VMEM((3, plane, size_z), f32),
        ],
        compiler_params=pltpu.CompilerParams(vmem_limit_bytes=40 * 1024 * 1024),
    )(counts, pick, state, slots, contacts, holder, coefs, fluid, solid)


def per_device(
    populations,
    solid,
    coefficients,
    body_nodes,
    centers,
    angles,
    velocity,
    node_frac,
    node_cell,
    grain_tile,
    send_grain,
    recv_partner,
):
    directions, size_x, size_y, size_z = populations.shape
    plane = size_x * size_y
    grains = centers.shape[1]
    nodes = body_nodes.shape[1]
    count_z = lax.axis_size("gz")
    owners = lax.axis_size("gx") * count_z
    tile_cap = max(2, 2 * grains // owners)
    tile_slots = owners * tile_cap
    contact_slots = send_grain.shape[1]
    contact_cap = contact_slots // owners
    me = lax.axis_index("gx") * count_z + lax.axis_index("gz")
    first = (me * grains).astype(f32)

    route = grain_tile[0, :, 0]
    hot = (route[:, None] == jnp.arange(owners, dtype=jnp.int32)[None, :]).astype(jnp.int32)
    below = np.tril(np.ones((grains, grains), np.int32), -1)
    earlier = (route[:, None] == route[None, :]) & (below > 0)
    rank = jnp.sum(earlier.astype(jnp.int32), axis=1)
    slot_of = route * tile_cap + rank
    match = slot_of[:, None] == jnp.arange(tile_slots, dtype=jnp.int32)[None, :]
    grain_ids = jnp.arange(grains, dtype=jnp.int32)
    slot_grain = jnp.sum(jnp.where(match, grain_ids[:, None] + 1, 0), axis=0) - 1
    chosen = jnp.concatenate(
        [slot_grain.reshape(owners, tile_cap), send_grain[0].reshape(owners, contact_cap)], axis=1
    ).reshape(-1)
    name = jnp.where(chosen >= 0, chosen.astype(f32) + first, -1.0)
    tiles = jnp.concatenate(
        [body_nodes, node_frac, node_cell.astype(f32)[None], jnp.zeros((1, nodes, grains), f32)]
    ).transpose(2, 0, 1)
    packed = pack(jnp.maximum(chosen, 0), name, tiles).reshape(owners, tile_cap + contact_cap, 8, nodes)
    small = jnp.concatenate([angles, centers, velocity]).reshape(-1)
    tile_size = 8 * nodes
    small_tiles = -(-small.shape[0] // tile_size)
    small = jnp.pad(small, (0, small_tiles * tile_size - small.shape[0])).reshape(1, small_tiles, 8, nodes)
    small = jnp.broadcast_to(small, (owners, small_tiles, 8, nodes))
    got = lax.all_to_all(
        jnp.concatenate([packed, small], axis=1), ("gx", "gz"), split_axis=0, concat_axis=0, tiled=True
    )
    slots = got[:, :tile_cap].reshape(tile_slots, 8, nodes)
    contacts = got[:, tile_cap : tile_cap + contact_cap].reshape(contact_slots, 8, nodes)
    everyone = got[:, tile_cap + contact_cap :].reshape(owners, -1)[:, : 12 * grains]
    everyone = everyone.reshape(owners, 12, grains).transpose(1, 0, 2).reshape(12, owners * grains)
    counts = jnp.sum((slots[:, 7, 0].reshape(owners, tile_cap) >= 0.0).astype(jnp.int32), axis=1)
    recv = recv_partner[0]
    pick = jnp.maximum(recv, 0)
    holder = jnp.where(recv >= 0, recv.astype(f32) + first, -1.0)[:, None]

    rows = rotation_rows(everyone[0:3]) + [everyone[3 + i] for i in range(9)]
    state = jnp.stack(rows)
    solid_flat = solid.reshape(plane, size_z)
    fluid = populations
    for step in range(STEPS):
        post, loads = run_step(
            size_y,
            tile_cap,
            counts,
            pick,
            state,
            slots,
            contacts,
            holder,
            coefficients,
            fluid.reshape(directions, plane, size_z),
            solid_flat,
        )
        totals = lax.psum(loads, ("gx", "gy", "gz"))
        fluid = stream(post.reshape(populations.shape), solid)
        if step == STEPS - 1:
            state = lax.dynamic_slice_in_dim(state, me * grains, grains, axis=1)
            totals = lax.dynamic_slice_in_dim(totals, me * grains, grains, axis=1)
        state = jnp.stack(advance_rows([state[i] for i in range(18)], [totals[i] for i in range(6)]))
    return (fluid, state[9:12], state[12:18])


def solution(mesh):
    in_specs = (
        P(None, "gx", "gy", "gz"),
        P("gx", "gy", "gz"),
        P(("gx", "gz"), None, None),
        P(None, "gy", ("gx", "gz")),
        P(None, ("gx", "gz")),
        P(None, ("gx", "gz")),
        P(None, ("gx", "gz")),
        P(None, "gy", ("gx", "gz")),
        P("gy", ("gx", "gz")),
        P("gy", ("gx", "gz"), None),
        P(("gx", "gz"), None),
        P(("gx", "gz"), None),
    )
    out_specs = (P(None, "gx", "gy", "gz"), P(None, ("gx", "gz")), P(None, ("gx", "gz")))
    return jax.shard_map(
        per_device, mesh=mesh, in_specs=in_specs, out_specs=out_specs, check_vma=False
    )
```

profile of v0, /device:TPU:0, one launch (start us, length us, event | category | flops | bytes accessed | tf_op | source)
XLA Modules:
  0.0 202.3 jit_solution(3491317211605088841)
XLA Ops:
  0.7 0.8 pad_maximum_fusion.5
  2.0 1.3 reduce.65
  3.4 0.9 convert_reduce_fusion
  4.3 0.7 iota_add_fusion
  5.3 0.7 max.11.index_ref
  6.0 0.6 select_n.79.name_ref
  6.7 0.8 copy-done.5
  7.7 0.8 maximum_bitcast_fusion.tiles_ref
  8.5 2.1 %shard_map.391 = f32[160,8,128]{2,1,0:T(8,128)} custom-call(s32[160]{0:T(256)} %max.11.index_ref, f32[160]{0:T(256)} %select_n.79.name_ref, f32[64,8,128]{2,1,0:T(8,128)} %maximum_bitcast_fusion.tiles_ref), custom_call_target="tpu_custom_call" | custom-call | tf_op jit(solution)/shard_map/pallas_call | solution.py:144
  10.6 2.0 pad_maximum_fusion
  12.6 5.3 %all-to-all-start = ((f32[8,21,8,128]{3,2,1,0:T(8,128)}), f32[8,21,8,128]{3,2,1,0:T(8,128)S(1)}, u32[]{:S(2)}, u32[]{:S(2)}) async-start(f32[8,21,8,128]{3,2,1,0:T(8,128)} %pad_maximum_fusion), calls=%async_computation | async-start | bytes 1376256 | tf_op jit(solution)/shard_map/all_to_all | solution.py:494
  18.0 0.6 copy-done.9
  19.5 9.9 %all-to-all-done = f32[8,21,8,128]{3,2,1,0:T(8,128)S(1)} async-done(((f32[8,21,8,128]{3,2,1,0:T(8,128)}), f32[8,21,8,128]{3,2,1,0:T(8,128)S(1)}, u32[]{:S(2)}, u32[]{:S(2)}) %all-to-all-start) | async-done | bytes 688160 | tf_op jit(solution)/shard_map/all_to_all | solution.py:494
  29.5 2.4 %fusion = s32[128]{0:T(128)S(1)} fusion(f32[128,8,128]{2,1,0:T(8,128)S(1)} %bitcast.271), kind=kLoop, calls=%fused_computation.91 | loop fusion | flops 256 | bytes 1024 | tf_op jit(solution)/shard_map/convert_element_type | solution.py:501
  34.0 0.9 slice.769
  34.9 15.1 %shard_map.392 = (f32[19,64,128]{2,1,0:T(8,128)S(1)}, f32[8,512]{1,0:T(8,128)S(1)}) custom-call(s32[8]{0:T(128)S(1)} %reduce_sum.29.counts_ref, s32[32]{0:T(128)S(1)} %maximum_bitcast_fusion.1.pick_ref, f32[18,512]{1,0:T(8,128)S(1)} %stack.100.state_ref, f32[128,8,128]{2,1,0:T(8,128)S(1)} %bitcast.272, f32[32,8,128]{2,1,0:T(8,128)S(1)} %bitcast.275, ...), custom_call_target="tpu_custom_call" | custom-call | tf_op jit(solution)/shard_map/pallas_call | solution.py:424
  50.0 45.9 %psum.14 = f32[8,512]{1,0:T(8,128)S(1)} all-reduce(f32[8,512]{1,0:T(8,128)S(1)} %get-tuple-element.7), channel_id=1, replica_groups=mesh['gx'=4,'gy'=4,'gz'=2] {'gx','gy','gz'}, use_global_device_ids=true, to_apply=%region_3.4 | all-reduce | flops 4096 | bytes 32768 | tf_op jit(solution)/shard_map/psum | solution.py:524
  96.4 2.3 %collective-permute-start = (f32[10,1,16,128]{3,2,1,0:T(8,128)S(1)}, f32[10,1,16,128]{3,2,1,0:T(8,128)S(1)}, u32[]{:S(2)}, u32[]{:S(2)}) collective-permute-start(f32[10,1,16,128]{3,2,1,0:T(8,128)S(1)} %get-tuple-element.96), channel_id=1, source_target_pairs={{0,8},{8,16},{16,24},{24,0},{1,9},{9,17},{17,25},{25,1},{2,10},{10... | collective-permute-start | bytes 245768 | tf_op jit(solution)/shard_map/ppermute | solution.py:58
  98.8 1.7 collective-permute-start.1
  100.5 2.1 %collective-permute-done = f32[10,1,16,128]{3,2,1,0:T(8,128)S(1)} collective-permute-done((f32[10,1,16,128]{3,2,1,0:T(8,128)S(1)}, f32[10,1,16,128]{3,2,1,0:T(8,128)S(1)}, u32[]{:S(2)}, u32[]{:S(2)}) %collective-permute-start) | collective-permute-done | bytes 81952 | tf_op jit(solution)/shard_map/ppermute | solution.py:58
  102.7 1.1 collective-permute-done.1
  103.9 1.0 scatter_fusion
  105.6 2.3 %collective-permute-start.3 = (f32[10,4,1,128]{3,2,1,0:T(1,128)S(1)}, f32[10,4,1,128]{3,2,1,0:T(1,128)S(1)}, u32[]{:S(2)}, u32[]{:S(2)}) collective-permute-start(f32[10,4,1,128]{3,2,1,0:T(1,128)S(1)} %get-tuple-element.94), channel_id=1, source_target_pairs={{2,0},{4,2},{6,4},{0,6},{3,1},{5,3},{7,5},{1,7},{10,8},{12,10},{14... | collective-permute-start | bytes 61448 | tf_op jit(solution)/shard_map/ppermute | solution.py:60
  107.8 1.6 collective-permute-done.3
  109.4 4.0 %collective-permute-done.2 = f32[10,4,1,128]{3,2,1,0:T(1,128)S(1)} collective-permute-done((f32[10,4,1,128]{3,2,1,0:T(1,128)S(1)}, f32[10,4,1,128]{3,2,1,0:T(1,128)S(1)}, u32[]{:S(2)}, u32[]{:S(2)}) %collective-permute-start.2) | collective-permute-done | bytes 20512 | tf_op jit(solution)/shard_map/ppermute | solution.py:58
  113.7 1.0 scatter_fusion.1
  116.2 1.1 collective-permute-done.5
  117.7 1.4 pad_maximum_fusion.1
  119.6 1.0 scatter_fusion.2
  120.7 0.6 gather_fusion.3
  121.3 15.1 %shard_map.393 = (f32[19,64,128]{2,1,0:T(8,128)S(1)}, f32[8,512]{1,0:T(8,128)S(1)}) custom-call(s32[8]{0:T(128)S(1)} %reduce_sum.29.counts_ref, s32[32]{0:T(128)S(1)} %maximum_bitcast_fusion.1.pick_ref, f32[18,512]{1,0:T(8,128)S(1)} %stack.101.state_ref, f32[128,8,128]{2,1,0:T(8,128)S(1)} %bitcast.273, f32[32,8,128]{2,1,0:T(8,128)S(1)} %bitcast.276, ...), custom_call_target="tpu_custom_call" | custom-call | tf_op jit(solution)/shard_map/pallas_call | solution.py:424
  137.0 4.3 %collective-permute-start.6 = (f32[10,1,16,128]{3,2,1,0:T(8,128)S(1)}, f32[10,1,16,128]{3,2,1,0:T(8,128)S(1)}, u32[]{:S(2)}, u32[]{:S(2)}) collective-permute-start(f32[10,1,16,128]{3,2,1,0:T(8,128)S(1)} %get-tuple-element.88), channel_id=1, source_target_pairs={{0,8},{8,16},{16,24},{24,0},{1,9},{9,17},{17,25},{25,1},{2,10},{10... | collective-permute-start | bytes 245768 | tf_op jit(solution)/shard_map/ppermute | solution.py:58
  141.3 42.2 %psum.15 = f32[8,512]{1,0:T(8,128)S(1)} all-reduce(f32[8,512]{1,0:T(8,128)S(1)} %get-tuple-element.10), channel_id=1, replica_groups=mesh['gx'=4,'gy'=4,'gz'=2] {'gx','gy','gz'}, use_global_device_ids=true, to_apply=%region_10.11 | all-reduce | flops 4096 | bytes 32768 | tf_op jit(solution)/shard_map/psum | solution.py:524
  183.8 0.6 copy-done.12
  184.5 1.0 scatter_fusion.3
  185.5 0.6 gather_fusion.5
  186.1 2.4 %collective-permute-start.9 = (f32[10,4,1,128]{3,2,1,0:T(1,128)S(1)}, f32[10,4,1,128]{3,2,1,0:T(1,128)S(1)}, u32[]{:S(2)}, u32[]{:S(2)}) collective-permute-start(f32[10,4,1,128]{3,2,1,0:T(1,128)S(1)} %get-tuple-element.86), channel_id=1, source_target_pairs={{2,0},{4,2},{6,4},{0,6},{3,1},{5,3},{7,5},{1,7},{10,8},{12,10},{14... | collective-permute-start | bytes 61448 | tf_op jit(solution)/shard_map/ppermute | solution.py:60
  188.5 0.6 collective-permute-start.8
  189.2 1.6 collective-permute-done.9
  190.8 3.2 %collective-permute-done.8 = f32[10,4,1,128]{3,2,1,0:T(1,128)S(1)} collective-permute-done((f32[10,4,1,128]{3,2,1,0:T(1,128)S(1)}, f32[10,4,1,128]{3,2,1,0:T(1,128)S(1)}, u32[]{:S(2)}, u32[]{:S(2)}) %collective-permute-start.8) | collective-permute-done | bytes 20512 | tf_op jit(solution)/shard_map/ppermute | solution.py:58
  194.3 0.6 copy-done.10
  195.0 1.0 scatter_fusion.4
  196.0 0.6 gather_fusion.6
  197.3 0.6 pad_maximum_fusion.6
  197.9 0.6 stack.264
  199.7 1.0 scatter_fusion.5
  200.7 0.6 gather_fusion.7
  201.3 0.9 broadcast_select_fusion
  (172 shorter events, 11.2 us)
Async XLA Ops:
  0.6 2.8 %copy-start.7 = (pred[64,64]{1,0:T(32,128)(4,1)S(1)}, pred[64,64]{1,0:T(32,128)(4,1)}, u32[]{:S(2)}) copy-start(pred[64,64]{1,0:T(32,128)(4,1)} %constant.16.clone) | copy-start | bytes 12292
  0.6 6.0 %copy-start.6 = (s32[128,64]{0,1:T(8,128)S(1)}, s32[128,64]{0,1:T(8,128)}, u32[]{:S(2)}) copy-start(s32[128,64]{0,1:T(8,128)} %param.48) | copy-start | bytes 98308
  0.7 6.0 %copy-start.4 = (f32[3,128,64]{1,2,0:T(8,128)S(1)}, f32[3,128,64]{1,2,0:T(8,128)}, u32[]{:S(2)}) copy-start(f32[3,128,64]{1,2,0:T(8,128)} %param.47) | copy-start | bytes 294916
  6.7 0.9 copy-start.5
  12.6 5.3 %copy-start.14 = (s32[1,32]{1,0:T(1,128)S(1)}, s32[1,32]{1,0:T(1,128)}, u32[]{:S(2)}) copy-start(s32[1,32]{1,0:T(1,128)} %param.51) | copy-start | bytes 388
  12.6 16.8 %all-to-all-start = ((f32[8,21,8,128]{3,2,1,0:T(8,128)}), f32[8,21,8,128]{3,2,1,0:T(8,128)S(1)}, u32[]{:S(2)}, u32[]{:S(2)}) async-start(f32[8,21,8,128]{3,2,1,0:T(8,128)} %pad_maximum_fusion), calls=%async_computation | async-start | bytes 1376256 | tf_op jit(solution)/shard_map/all_to_all | solution.py:494
  17.9 0.7 copy-start.9
  17.9 0.7 copy-start.11
  18.6 0.7 copy-start.8
  18.6 0.7 copy-start.13
  18.7 0.8 copy-start.2
  18.7 16.2 %copy-start = (f32[64,16,256]{2,1,0:T(8,128)S(1)}, f32[64,16,256]{2,1,0:T(8,128)}, u32[]{:S(2)}) copy-start(f32[64,16,256]{2,1,0:T(8,128)} %coef_ref.3) | copy-start | bytes 3145732
  29.4 4.4 %copy-start.3 = (f32[8,21,8,128]{3,2,1,0:T(8,128)}, f32[8,21,8,128]{3,2,1,0:T(8,128)S(1)}, u32[]{:S(2)}) copy-start(f32[8,21,8,128]{3,2,1,0:T(8,128)S(1)} %all-to-all-done) | copy-start | bytes 2064388
  29.5 5.4 %copy-start.1 = (f32[19,4,16,128]{3,2,1,0:T(8,128)S(1)}, f32[19,4,16,128]{3,2,1,0:T(8,128)}, u32[]{:S(2)}) copy-start(f32[19,4,16,128]{3,2,1,0:T(8,128)} %param.40) | copy-start | bytes 1867780
  96.4 6.1 %collective-permute-start = (f32[10,1,16,128]{3,2,1,0:T(8,128)S(1)}, f32[10,1,16,128]{3,2,1,0:T(8,128)S(1)}, u32[]{:S(2)}, u32[]{:S(2)}) collective-permute-start(f32[10,1,16,128]{3,2,1,0:T(8,128)S(1)} %get-tuple-element.96), channel_id=1, source_target_pairs={{0,8},{8,16},{16,24},{24,0},{1,9},{9,17},{17,25},{25,1},{2,10},{10... | collective-permute-start | bytes 245768 | tf_op jit(solution)/shard_map/ppermute | solution.py:58
  98.8 5.0 %collective-permute-start.1 = (f32[10,1,16,128]{3,2,1,0:T(8,128)S(1)}, f32[10,1,16,128]{3,2,1,0:T(8,128)S(1)}, u32[]{:S(2)}, u32[]{:S(2)}) collective-permute-start(f32[10,1,16,128]{3,2,1,0:T(8,128)S(1)} %get-tuple-element.95), channel_id=1, source_target_pairs={{8,0},{16,8},{24,16},{0,24},{9,1},{17,9},{25,17},{1,25},{10,2},{18... | collective-permute-start | bytes 245768 | tf_op jit(solution)/shard_map/ppermute | solution.py:60
  105.6 3.8 %collective-permute-start.3 = (f32[10,4,1,128]{3,2,1,0:T(1,128)S(1)}, f32[10,4,1,128]{3,2,1,0:T(1,128)S(1)}, u32[]{:S(2)}, u32[]{:S(2)}) collective-permute-start(f32[10,4,1,128]{3,2,1,0:T(1,128)S(1)} %get-tuple-element.94), channel_id=1, source_target_pairs={{2,0},{4,2},{6,4},{0,6},{3,1},{5,3},{7,5},{1,7},{10,8},{12,10},{14... | collective-permute-start | bytes 61448 | tf_op jit(solution)/shard_map/ppermute | solution.py:60
  107.8 5.6 %collective-permute-start.2 = (f32[10,4,1,128]{3,2,1,0:T(1,128)S(1)}, f32[10,4,1,128]{3,2,1,0:T(1,128)S(1)}, u32[]{:S(2)}, u32[]{:S(2)}) collective-permute-start(f32[10,4,1,128]{3,2,1,0:T(1,128)S(1)} %get-tuple-element.93), channel_id=1, source_target_pairs={{0,2},{2,4},{4,6},{6,0},{1,3},{3,5},{5,7},{7,1},{8,10},{10,12},{12... | collective-permute-start | bytes 61448 | tf_op jit(solution)/shard_map/ppermute | solution.py:58
  115.4 1.8 collective-permute-start.5
  115.5 2.2 %collective-permute-start.4 = (f32[10,4,16,1]{3,2,1,0:T(8,128)S(1)}, f32[10,4,16,1]{3,2,1,0:T(8,128)}, u32[]{:S(2)}, u32[]{:S(2)}) collective-permute-start(f32[10,4,16,1]{3,2,1,0:T(8,128)S(1)} %get-tuple-element.91), channel_id=1, source_target_pairs={{0,1},{1,0},{2,3},{3,2},{4,5},{5,4},{6,7},{7,6},{8,9},{9,8},{10,11... | collective-permute-start | bytes 7688 | tf_op jit(solution)/shard_map/ppermute | solution.py:58
  137.0 46.6 %collective-permute-start.6 = (f32[10,1,16,128]{3,2,1,0:T(8,128)S(1)}, f32[10,1,16,128]{3,2,1,0:T(8,128)S(1)}, u32[]{:S(2)}, u32[]{:S(2)}) collective-permute-start(f32[10,1,16,128]{3,2,1,0:T(8,128)S(1)} %get-tuple-element.88), channel_id=1, source_target_pairs={{0,8},{8,16},{16,24},{24,0},{1,9},{9,17},{17,25},{25,1},{2,10},{10... | collective-permute-start | bytes 245768 | tf_op jit(solution)/shard_map/ppermute | solution.py:58
  141.3 42.4 %collective-permute-start.7 = (f32[10,1,16,128]{3,2,1,0:T(8,128)S(1)}, f32[10,1,16,128]{3,2,1,0:T(8,128)S(1)}, u32[]{:S(2)}, u32[]{:S(2)}) collective-permute-start(f32[10,1,16,128]{3,2,1,0:T(8,128)S(1)} %get-tuple-element.87), channel_id=1, source_target_pairs={{8,0},{16,8},{24,16},{0,24},{9,1},{17,9},{25,17},{1,25},{10,2},{18... | collective-permute-start | bytes 245768 | tf_op jit(solution)/shard_map/ppermute | solution.py:60
  183.8 0.7 copy-start.12
  186.1 4.7 %collective-permute-start.9 = (f32[10,4,1,128]{3,2,1,0:T(1,128)S(1)}, f32[10,4,1,128]{3,2,1,0:T(1,128)S(1)}, u32[]{:S(2)}, u32[]{:S(2)}) collective-permute-start(f32[10,4,1,128]{3,2,1,0:T(1,128)S(1)} %get-tuple-element.86), channel_id=1, source_target_pairs={{2,0},{4,2},{6,4},{0,6},{3,1},{5,3},{7,5},{1,7},{10,8},{12,10},{14... | collective-permute-start | bytes 61448 | tf_op jit(solution)/shard_map/ppermute | solution.py:60
  188.5 5.6 %collective-permute-start.8 = (f32[10,4,1,128]{3,2,1,0:T(1,128)S(1)}, f32[10,4,1,128]{3,2,1,0:T(1,128)S(1)}, u32[]{:S(2)}, u32[]{:S(2)}) collective-permute-start(f32[10,4,1,128]{3,2,1,0:T(1,128)S(1)} %get-tuple-element.85), channel_id=1, source_target_pairs={{0,2},{2,4},{4,6},{6,0},{1,3},{3,5},{5,7},{7,1},{8,10},{10,12},{12... | collective-permute-start | bytes 61448 | tf_op jit(solution)/shard_map/ppermute | solution.py:58
  194.3 0.7 copy-start.10
  196.7 1.8 collective-permute-start.11
  196.8 2.1 %collective-permute-start.10 = (f32[10,4,16,1]{3,2,1,0:T(8,128)S(1)}, f32[10,4,16,1]{3,2,1,0:T(8,128)S(1)}, u32[]{:S(2)}, u32[]{:S(2)}) collective-permute-start(f32[10,4,16,1]{3,2,1,0:T(8,128)S(1)} %get-tuple-element.83), channel_id=1, source_target_pairs={{0,1},{1,0},{2,3},{3,2},{4,5},{5,4},{6,7},{7,6},{8,9},{9,8},{10,11... | collective-permute-start | bytes 7688 | tf_op jit(solution)/shard_map/ppermute | solution.py:58
where the time goes:
time: 205 us; the launch traced here: 202 us
  blocking collectives  88.1 us (43%)
  Pallas kernels  32.3 us (16%)
  waiting for transfers between devices  25.6 us (12%)
  local copies, waits for them, and re-layouts  22 us (11%)
  starting transfers between devices  20 us (10%)
  other arithmetic  12.9 us (6%)
    psum x2, blocking collectives, per_device(): totals = lax.psum(loads, ('gx', 'gy', 'gz'))  88.1 us
    pallas_call x2, Pallas kernels, run_step(): pl.pallas_call(functools.partial(step_kernel, size_y, tile_cap, math.gcd(...  30.1 us
    ppermute x6, waiting for transfers between devices, padded_2(): lax.ppermute(tail, axis, [(i, (i + 1) % count) for i in range(count)])  10.2 us
    all_to_all x1, waiting for transfers between devices, per_device(): lax.all_to_all(jnp.concatenate([packed, small], axis=1), ('gx', 'gz'), sp...  9.94 us
    ppermute x6, starting transfers between devices, padded_2(): lax.ppermute(tail, axis, [(i, (i + 1) % count) for i in range(count)])  8.26 us
    ppermute x6, starting transfers between devices, padded_2(): lax.ppermute(head, axis, [((i + 1) % count, i) for i in range(count)])  6.42 us
    scatter x6, local copies, waits for them, and re-layouts, stream(): moved = moved.at[np.array(chosen, dtype=np.int32)].set(jnp.stack(shifted))  6.15 us
    ppermute x6, waiting for transfers between devices, padded_2(): lax.ppermute(head, axis, [((i + 1) % count, i) for i in range(count)])  5.43 us
  transfers between devices with their start and end apart: 13, of which 10 were waited for; matrix products, arithmetic and copies ran while one was open for 1% of the time, Pallas kernels for 0%

commit v1 on v0

--- a/solution.py
+++ b/solution.py
@@ -37,52 +37,13 @@
     dtype=np.int32,
 )
 lattice_weights = [1.0 / 3.0] + [1.0 / 18.0] * 6 + [1.0 / 36.0] * 12
-opposite_dirs = np.array(
-    [0, 2, 1, 4, 3, 6, 5, 8, 7, 10, 9, 12, 11, 14, 13, 16, 15, 18, 17], dtype=np.int32
-)
 tau_relax = 0.9
 ib_stiffness = 0.5
 contact_stiffness = 0.05
 time_step = 0.05
 bf16 = jnp.bfloat16
 f32 = jnp.float32
-
-
-def padded_2(cells, sides, width):
-    for axis, dim in sides:
-        count = lax.axis_size(axis)
-        head = lax.slice_in_dim(cells, 0, width, axis=dim)
-        tail = lax.slice_in_dim(cells, cells.shape[dim] - width, cells.shape[dim], axis=dim)
-        cells = jnp.concatenate(
-            [
-                lax.ppermute(tail, axis, [(i, (i + 1) % count) for i in range(count)]),
-                cells,
-                lax.ppermute(head, axis, [((i + 1) % count, i) for i in range(count)]),
-            ],
-            axis=dim,
-        )
-    return cells
-
-
-def stream(post, solid):
-    directions = post.shape[0]
-    moved = post
-    for axis_part, axis in enumerate(("gx", "gy", "gz")):
-        chosen = [d for d in range(directions) if lattice_dirs[d][axis_part] != 0]
-        selected = moved[np.array(chosen, dtype=np.int32)]
-        padded = padded_2(selected, ((axis, axis_part + 1),), 1)
-        extent = selected.shape[axis_part + 1]
-        shifted = [
-            lax.slice_in_dim(
-                padded[position],
-                1 - int(lattice_dirs[direction][axis_part]),
-                1 - int(lattice_dirs[direction][axis_part]) + extent,
-                axis=axis_part,
-            )
-            for position, direction in enumerate(chosen)
-        ]
-        moved = moved.at[np.array(chosen, dtype=np.int32)].set(jnp.stack(shifted))
-    return jnp.where(solid[None] > 0, moved[opposite_dirs], moved)
+MESH = pl.DeviceIdType.MESH
 
 
 def rotation_rows(angles):
@@ -129,28 +90,321 @@
     return high, (values - high.astype(f32)).astype(bf16)
 
 
-def pack_kernel(index_ref, name_ref, tiles_ref, out_ref):
+def other(axis, step):
+    count = lax.axis_size(axis)
+    return lax.rem(lax.axis_index(axis) + (step + count), count)
+
+
+def place(step_x, step_y, step_z):
+    return (other("gx", step_x), other("gy", step_y), other("gz", step_z))
+
+
+def owner_index():
+    return lax.axis_index("gx") * lax.axis_size("gz") + lax.axis_index("gz")
+
+
+def owner_place(step):
+    count_z = lax.axis_size("gz")
+    owners = lax.axis_size("gx") * count_z
+    owner = lax.rem(owner_index() + step, owners)
+    return owner, (lax.div(owner, count_z), lax.axis_index("gy"), lax.rem(owner, count_z))
+
+
+def greet(places):
+    barrier = pltpu.get_barrier_semaphore()
+    for device in places:
+        pl.semaphore_signal(barrier, inc=1, device_id=device, device_id_type=MESH)
+    pl.semaphore_wait(barrier, len(places))
+
+
+def remote(source, target, send, receive, device):
+    copy = pltpu.make_async_remote_copy(
+        src_ref=source,
+        dst_ref=target,
+        send_sem=send,
+        recv_sem=receive,
+        device_id=device,
+        device_id_type=MESH,
+    )
+    copy.start()
+    return copy
+
+
+def deal_kernel(
+    owners,
+    index_ref,
+    name_ref,
+    tiles_ref,
+    small_ref,
+    slots_ref,
+    contacts_ref,
+    all_ref,
+    out_slots,
+    out_contacts,
+    send_sem,
+    recv_sem,
+):
+    cap, contact_cap = slots_ref.shape[1], contacts_ref.shape[1]
+    width = cap + contact_cap
     row = lax.broadcasted_iota(jnp.int32, tiles_ref.shape[1:], 0)
-
-    def body(slot, carry):
-        tile = tiles_ref[index_ref[slot]]
-        out_ref[slot] = jnp.where(row == 7, name_ref[slot], tile)
-        return carry
-
-    lax.fori_loop(0, out_ref.shape[0], body, 0, unroll=8)
-
-
-def pack(index, name, tiles):
+    me = owner_index()
+
+    def fill(k, owner, slots, contacts):
+        for r in range(width):
+            at = owner * width + r
+            tile = jnp.where(row == 7, name_ref[at], tiles_ref[index_ref[at]])
+            if r < cap:
+                slots[k, r] = tile
+            else:
+                contacts[k, r - cap] = tile
+
+    greet([owner_place(k)[1] for k in range(1, owners)])
+    copies = []
+    for k in range(1, owners):
+        owner, device = owner_place(k)
+        fill(k, owner, out_slots, out_contacts)
+        pairs = (
+            (out_slots.at[k], slots_ref.at[me]),
+            (out_contacts.at[k], contacts_ref.at[me]),
+            (small_ref, all_ref.at[me]),
+        )
+        for i, (source, target) in enumerate(pairs):
+            copies.append(remote(source, target, send_sem.at[i, k], recv_sem.at[i, k], device))
+    fill(me, me, slots_ref, contacts_ref)
+    all_ref[me] = small_ref[...]
+    for copy in copies:
+        copy.wait()
+
+
+def deal(owners, cap, index, name, tiles, small):
+    nodes = tiles.shape[2]
+    contact_cap = index.shape[0] // owners - cap
+    vmem = pl.BlockSpec(memory_space=pltpu.VMEM)
+    smem = pl.BlockSpec(memory_space=pltpu.SMEM)
+    slots = (owners, cap, 8, nodes)
+    contacts = (owners, contact_cap, 8, nodes)
     return pl.pallas_call(
-        pack_kernel,
-        out_shape=jax.ShapeDtypeStruct((index.shape[0],) + tiles.shape[1:], f32),
-        in_specs=[
-            pl.BlockSpec(memory_space=pltpu.SMEM),
-            pl.BlockSpec(memory_space=pltpu.SMEM),
-            pl.BlockSpec(memory_space=pltpu.VMEM),
+        functools.partial(deal_kernel, owners),
+        out_shape=(
+            jax.ShapeDtypeStruct(slots, f32),
+            jax.ShapeDtypeStruct(contacts, f32),
+            jax.ShapeDtypeStruct((owners,) + small.shape, f32),
+        ),
+        in_specs=[smem, smem, vmem, vmem],
+        out_specs=(vmem, vmem, vmem),
+        scratch_shapes=[
+            pltpu.VMEM(slots, f32),
+            pltpu.VMEM(contacts, f32),
+            pltpu.SemaphoreType.DMA((3, owners)),
+            pltpu.SemaphoreType.DMA((3, owners)),
         ],
-        out_specs=pl.BlockSpec(memory_space=pltpu.VMEM),
-    )(index, name, tiles)
+        compiler_params=pltpu.CompilerParams(
+            collective_id=0, has_side_effects=True, vmem_limit_bytes=40 * 1024 * 1024
+        ),
+    )(index, name, tiles, small)
+
+
+def moving(axis, way):
+    return [q for q in range(19) if lattice_dirs[q][axis] == way]
+
+
+corners = [(1, 1), (-1, -1), (1, -1), (-1, 1)]
+
+
+def corner_dir(way_x, way_y):
+    return [q for q in range(19) if tuple(lattice_dirs[q]) == (way_x, way_y, 0)][0]
+
+
+def exchange_kernel(
+    owners,
+    count_y,
+    size_y,
+    post_ref,
+    solid_ref,
+    loads_ref,
+    state_ref,
+    fluid_ref,
+    next_ref,
+    depth_ref,
+    z_out,
+    z_in,
+    x_out,
+    x_in,
+    y_out,
+    y_in,
+    corner_out,
+    corner_in,
+    owner_in,
+    owner_sum,
+    slab_in,
+    send_sem,
+    recv_sem,
+    owner_send,
+    owner_recv,
+    slab_send,
+    slab_recv,
+):
+    directions, plane, size_z = post_ref.shape
+    size_x = plane // size_y
+    ways = (1, -1)
+    me = owner_index()
+    greet(
+        [owner_place(k)[1] for k in range(1, owners)]
+        + [place(0, k, 0) for k in range(1, count_y)]
+        + [place(way_x, way_y, 0) for way_x, way_y in corners]
+    )
+    owner_copies = [
+        remote(loads_ref, owner_in.at[k], owner_send.at[k], owner_recv.at[k], owner_place(k)[1])
+        for k in range(1, owners)
+    ]
+    owner_in[0] = loads_ref[...]
+    lane = lax.broadcasted_iota(jnp.int32, (plane, size_z), 1)
+    z_copies = []
+    for i, way in enumerate(ways):
+        packed = jnp.zeros((plane, size_z), f32)
+        for p, q in enumerate(moving(2, way)):
+            shift = (p + 1) % size_z if way > 0 else p
+            values = post_ref[q]
+            if shift:
+                values = pltpu.roll(values, shift, 1)
+            packed = jnp.where(lane == p, values, packed)
+        z_out[i] = packed
+        z_copies.append(remote(z_out.at[i], z_in.at[i], send_sem.at[i], recv_sem.at[i], place(0, 0, way)))
+    for copy in z_copies:
+        copy.wait()
+    slot_of = {}
+    for i, way in enumerate(ways):
+        packed = z_in[i]
+        for p, q in enumerate(moving(2, way)):
+            slot_of[q] = len(slot_of)
+            edge = 0 if way > 0 else size_z - 1
+            shift = (edge - p) % size_z
+            face = pltpu.roll(packed, shift, 1) if shift else packed
+            rolled = pltpu.roll(post_ref[q], way % size_z, 1)
+            depth_ref[slot_of[q]] = jnp.where(lane == edge, face, rolled)
+
+    def block(q, x):
+        rows = pl.ds(x * size_y, size_y)
+        return depth_ref[slot_of[q], rows] if q in slot_of else post_ref[q, rows]
+
+    copies = []
+    for i, way in enumerate(ways):
+        for p, q in enumerate(moving(0, way)):
+            x_out[i, p] = block(q, size_x - 1 if way > 0 else 0)
+        copies.append(
+            remote(x_out.at[i], x_in.at[i], send_sem.at[2 + i], recv_sem.at[2 + i], place(way, 0, 0))
+        )
+    for i, way in enumerate(ways):
+        edge = size_y - 1 if way > 0 else 0
+        for p, q in enumerate(moving(1, way)):
+            for x in range(size_x):
+                y_out[i, p, x : x + 1] = block(q, x)[edge : edge + 1]
+        copies.append(
+            remote(y_out.at[i], y_in.at[i], send_sem.at[4 + i], recv_sem.at[4 + i], place(0, way, 0))
+        )
+    for i, (way_x, way_y) in enumerate(corners):
+        edge = size_y - 1 if way_y > 0 else 0
+        values = block(corner_dir(way_x, way_y), size_x - 1 if way_x > 0 else 0)
+        corner_out[i] = jnp.broadcast_to(values[edge : edge + 1], (8, size_z))
+        copies.append(
+            remote(
+                corner_out.at[i],
+                corner_in.at[i],
+                send_sem.at[6 + i],
+                recv_sem.at[6 + i],
+                place(way_x, way_y, 0),
+            )
+        )
+
+    for copy in owner_copies:
+        copy.wait()
+    added = owner_in[me]
+    for j in range(1, owners):
+        added = added + owner_in[lax.rem(me - j + owners, owners)]
+    owner_sum[...] = added
+    slab_copies = [
+        remote(owner_sum, slab_in.at[k], slab_send.at[k], slab_recv.at[k], place(0, k, 0))
+        for k in range(1, count_y)
+    ]
+    slab_in[0] = added
+
+    for copy in copies:
+        copy.wait()
+    y_row = lax.broadcasted_iota(jnp.int32, (size_y, size_z), 0)
+
+    def moved(q, x):
+        way_x, way_y = int(lattice_dirs[q][0]), int(lattice_dirs[q][1])
+        from_x = x - way_x
+        outside = from_x < 0 or from_x >= size_x
+        if outside:
+            values = x_in[ways.index(way_x), moving(0, way_x).index(q)]
+        else:
+            values = block(q, from_x)
+        if way_y:
+            if outside:
+                line = corner_in[corners.index((way_x, way_y))][0:1]
+            else:
+                line = y_in[ways.index(way_y), moving(1, way_y).index(q)][from_x : from_x + 1]
+            edge = 0 if way_y > 0 else size_y - 1
+            values = jnp.where(y_row == edge, line, pltpu.roll(values, way_y % size_y, 0))
+        return values
+
+    for x in range(size_x):
+        rows = pl.ds(x * size_y, size_y)
+        wall = solid_ref[rows] > 0
+        fluid_ref[0, rows] = moved(0, x)
+        for q in range(1, directions, 2):
+            here, there = moved(q, x), moved(q + 1, x)
+            fluid_ref[q, rows] = jnp.where(wall, there, here)
+            fluid_ref[q + 1, rows] = jnp.where(wall, here, there)
+
+    for copy in slab_copies:
+        copy.wait()
+    slab = lax.axis_index("gy")
+    added = slab_in[slab]
+    for j in range(1, count_y):
+        added = added + slab_in[lax.rem(slab - j + count_y, count_y)]
+    values = state_ref[...]
+    after = advance_rows([values[i : i + 1] for i in range(18)], [added[i : i + 1] for i in range(6)])
+    for i in range(18):
+        next_ref[i : i + 1] = after[i]
+
+
+def exchange(owners, count_y, size_y, post, solid, loads, state):
+    directions, plane, size_z = post.shape
+    size_x = plane // size_y
+    vmem = pl.BlockSpec(memory_space=pltpu.VMEM)
+    sides = len(moving(0, 1))
+    dma = pltpu.SemaphoreType.DMA
+    return pl.pallas_call(
+        functools.partial(exchange_kernel, owners, count_y, size_y),
+        out_shape=(jax.ShapeDtypeStruct(post.shape, f32), jax.ShapeDtypeStruct(state.shape, f32)),
+        in_specs=[vmem] * 4,
+        out_specs=(vmem, vmem),
+        scratch_shapes=[
+            pltpu.VMEM((2 * sides, plane, size_z), f32),
+            pltpu.VMEM((2, plane, size_z), f32),
+            pltpu.VMEM((2, plane, size_z), f32),
+            pltpu.VMEM((2, sides, size_y, size_z), f32),
+            pltpu.VMEM((2, sides, size_y, size_z), f32),
+            pltpu.VMEM((2, sides, size_x, size_z), f32),
+            pltpu.VMEM((2, sides, size_x, size_z), f32),
+            pltpu.VMEM((4, 8, size_z), f32),
+            pltpu.VMEM((4, 8, size_z), f32),
+            pltpu.VMEM((owners,) + loads.shape, f32),
+            pltpu.VMEM(loads.shape, f32),
+            pltpu.VMEM((count_y,) + loads.shape, f32),
+            dma((10,)),
+            dma((10,)),
+            dma((owners,)),
+            dma((owners,)),
+            dma((count_y,)),
+            dma((count_y,)),
+        ],
+        compiler_params=pltpu.CompilerParams(
+            collective_id=1, has_side_effects=True, vmem_limit_bytes=40 * 1024 * 1024
+        ),
+    )(post, solid, loads, state)
 
 
 def columns(matrix, count):
@@ -485,28 +739,19 @@
     tiles = jnp.concatenate(
         [body_nodes, node_frac, node_cell.astype(f32)[None], jnp.zeros((1, nodes, grains), f32)]
     ).transpose(2, 0, 1)
-    packed = pack(jnp.maximum(chosen, 0), name, tiles).reshape(owners, tile_cap + contact_cap, 8, nodes)
-    small = jnp.concatenate([angles, centers, velocity]).reshape(-1)
-    tile_size = 8 * nodes
-    small_tiles = -(-small.shape[0] // tile_size)
-    small = jnp.pad(small, (0, small_tiles * tile_size - small.shape[0])).reshape(1, small_tiles, 8, nodes)
-    small = jnp.broadcast_to(small, (owners, small_tiles, 8, nodes))
-    got = lax.all_to_all(
-        jnp.concatenate([packed, small], axis=1), ("gx", "gz"), split_axis=0, concat_axis=0, tiled=True
-    )
-    slots = got[:, :tile_cap].reshape(tile_slots, 8, nodes)
-    contacts = got[:, tile_cap : tile_cap + contact_cap].reshape(contact_slots, 8, nodes)
-    everyone = got[:, tile_cap + contact_cap :].reshape(owners, -1)[:, : 12 * grains]
-    everyone = everyone.reshape(owners, 12, grains).transpose(1, 0, 2).reshape(12, owners * grains)
+    rows = rotation_rows(angles) + [centers[i] for i in range(3)] + [velocity[i] for i in range(6)]
+    small = jnp.pad(jnp.stack(rows), ((0, 6), (0, -grains % 128)))
+    slots, contacts, everyone = deal(owners, tile_cap, jnp.maximum(chosen, 0), name, tiles, small)
+    slots = slots.reshape(tile_slots, 8, nodes)
+    contacts = contacts.reshape(contact_slots, 8, nodes)
+    state = everyone[:, :18, :grains].transpose(1, 0, 2).reshape(18, owners * grains)
     counts = jnp.sum((slots[:, 7, 0].reshape(owners, tile_cap) >= 0.0).astype(jnp.int32), axis=1)
     recv = recv_partner[0]
     pick = jnp.maximum(recv, 0)
     holder = jnp.where(recv >= 0, recv.astype(f32) + first, -1.0)[:, None]
 
-    rows = rotation_rows(everyone[0:3]) + [everyone[3 + i] for i in range(9)]
-    state = jnp.stack(rows)
     solid_flat = solid.reshape(plane, size_z)
-    fluid = populations
+    fluid = populations.reshape(directions, plane, size_z)
     for step in range(STEPS):
         post, loads = run_step(
             size_y,
@@ -518,16 +763,12 @@
             contacts,
             holder,
             coefficients,
-            fluid.reshape(directions, plane, size_z),
+            fluid,
             solid_flat,
         )
-        totals = lax.psum(loads, ("gx", "gy", "gz"))
-        fluid = stream(post.reshape(populations.shape), solid)
-        if step == STEPS - 1:
-            state = lax.dynamic_slice_in_dim(state, me * grains, grains, axis=1)
-            totals = lax.dynamic_slice_in_dim(totals, me * grains, grains, axis=1)
-        state = jnp.stack(advance_rows([state[i] for i in range(18)], [totals[i] for i in range(6)]))
-    return (fluid, state[9:12], state[12:18])
+        fluid, state = exchange(owners, lax.axis_size("gy"), size_y, post, solid_flat, loads, state)
+    state = lax.dynamic_slice_in_dim(state, me * grains, grains, axis=1)
+    return (fluid.reshape(populations.shape), state[9:12], state[12:18])
 
 
 def solution(mesh):

time: 205 us -> 98.1 us (0.48); the launches traced: 202 us -> 98 us
  blocking collectives: 88.1 us -> 0 us
  Pallas kernels: 32.3 us -> 84.6 us
  waiting for transfers between devices: 25.6 us -> 0 us
  starting transfers between devices: 20 us -> 0 us
  local copies, waits for them, and re-layouts: 22 us -> 5.77 us
  other arithmetic: 12.9 us -> 6.74 us
    psum x2 -> x0, blocking collectives: 88.1 us -> none  [per_device(): totals = lax.psum(loads, ('gx', 'gy', 'gz'))]
    pallas_call x1 -> x3, Pallas kernels: 2.12 us -> 58.6 us  [the longest x2 44.9 us: exchange(): pl.pallas_call(functools.partial(exchange_kernel, owners, count_y, size_y...]
    ppermute x12 -> x0, waiting for transfers between devices: 15.7 us -> none  [the longest x6 10.2 us: padded_2(): lax.ppermute(tail, axis, [(i, (i + 1) % count) for i in range(count)])]
    ppermute x12 -> x0, starting transfers between devices: 14.7 us -> none  [the longest x6 8.26 us: padded_2(): lax.ppermute(tail, axis, [(i, (i + 1) % count) for i in range(count)])]
    all_to_all x1 -> x0, waiting for transfers between devices: 9.94 us -> none  [per_device(): lax.all_to_all(jnp.concatenate([packed, small], axis=1), ('gx', 'gz'), sp...]
    scatter x6 -> x0, local copies, waits for them, and re-layouts: 6.15 us -> none  [stream(): moved = moved.at[np.array(chosen, dtype=np.int32)].set(jnp.stack(shifted))]
    all_to_all x1 -> x0, starting transfers between devices: 5.3 us -> none  [per_device(): lax.all_to_all(jnp.concatenate([packed, small], axis=1), ('gx', 'gz'), sp...]
    concatenate x6 -> x0, other arithmetic: 4.62 us -> none  [the longest x1 1.98 us: per_device(): jnp.concatenate([packed, small], axis=1)]
  transfers between devices with their start and end apart: 13 -> 0, of which waited for: 10 -> 0; matrix products, arithmetic and copies ran while one was open for 1% -> 0% of each run, Pallas kernels for 0% -> 0%
where the time goes in v1:
time: 98.1 us; the launch traced here: 98 us
  Pallas kernels  84.6 us (86%)
  other arithmetic  6.74 us (7%)
  local copies, waits for them, and re-layouts  5.77 us (6%)
    pallas_call x2, Pallas kernels, exchange(): pl.pallas_call(functools.partial(exchange_kernel, owners, count_y, size_y...  44.9 us
    pallas_call x2, Pallas kernels, run_step(): pl.pallas_call(functools.partial(step_kernel, size_y, tile_cap, math.gcd(...  26 us
    pallas_call x1, Pallas kernels, deal(): pl.pallas_call(functools.partial(deal_kernel, owners), out_shape=(jax.Sha...  13.7 us
    convert_element_type x1, other arithmetic, per_device(): (slots[:, 7, 0].reshape(owners, tile_cap) >= 0.0).astype(jnp.int32)  2.35 us
    unnamed x22, local copies, waits for them, and re-layouts  2.18 us

profile of v1, /device:TPU:0, one launch (start us, length us, event | category | flops | bytes accessed | tf_op | source)
XLA Modules:
  0.0 98.0 jit_solution(5207705946738964585)
XLA Ops:
  0.6 0.0 copy-start.6
  0.6 0.0 copy-start.3
  0.7 0.9 fusion.2
  1.5 0.0 copy-start.7
  1.5 0.0 copy-start.5
  1.5 0.0 copy-start.4
  1.5 0.8 fusion.5
  2.4 0.0 copy-start
  2.4 1.6 %stack.3 = f32[18,64]{1,0:T(8,128)S(1)} concatenate(f32[1,64]{1,0:T(1,128)S(1)} %fusion.5, f32[1,64]{1,0:T(1,128)S(1)} %get-tuple-element.31, f32[1,64]{1,0:T(1,128)S(1)} %get-tuple-element.30, f32[1,64]{1,0:T(1,128)S(1)} %get-tuple-element.26, f32[1,64]{1,0:T(1,128)S(1)} %get-tuple-element.28, f32[1,64]{1,0:T(1,128)S(1)} %get-tuple-element.32, f32[1,64]{1,0:T(1,128)S(1)} %get-tuple-element.29, ...), dimensions={0} | concatenate | bytes 9216 | tf_op jit(solution)/shard_map/stack | solution.py:743
  4.0 0.0 copy-done.6
  4.0 0.9 convert_reduce_fusion
  4.9 0.7 iota_add_fusion
  5.6 0.1 select_reduce_fusion
  5.7 0.1 sub.15
  5.7 0.5 broadcast.79
  6.3 0.0 copy-done.7
  6.3 0.7 reduce.5
  6.9 0.1 reshape_squeeze.4
  7.0 0.1 add_select_fusion
  7.1 0.1 select_n.29.name_ref
  7.2 0.1 broadcast_maximum_fusion
  7.2 0.1 max.11.index_ref
  7.3 0.0 copy-done.3
  7.3 0.1 copy.26
  7.4 0.0 copy-done.4
  7.4 0.1 copy.27
  7.5 0.0 copy-done.5
  7.5 0.1 pad.8.clone
  7.6 0.0 copy-start.1
  7.6 0.1 maximum_bitcast_fusion.tiles_ref
  7.7 13.7 %shard_map.148 = (f32[8,16,8,128]{3,2,1,0:T(8,128)S(1)}, f32[8,4,8,128]{3,2,1,0:T(8,128)S(1)}, f32[8,24,128]{2,1,0:T(8,128)S(1)}) custom-call(s32[160]{0:T(256)S(1)} %max.11.index_ref, f32[160]{0:T(256)S(1)} %select_n.29.name_ref, f32[64,8,128]{2,1,0:T(8,128)S(1)} %maximum_bitcast_fusion.tiles_ref, f32[24,128]{1,0:T(8,128)S(1)} %pad.4.small_ref), custom_call_target="tpu_custom_call" | custom-call | tf_op jit(solution)/shard_map/pallas_call | solution.py:186
  21.4 2.4 %fusion = s32[128]{0:T(128)S(1)} fusion(f32[128,8,128]{2,1,0:T(8,128)S(1)} %bitcast.17), kind=kLoop, calls=%fused_computation.3 | loop fusion | flops 256 | bytes 1024 | tf_op jit(solution)/shard_map/convert_element_type | solution.py:748
  23.7 0.1 reshape.97
  23.8 0.1 reduce_sum.29.counts_ref
  24.0 0.0 copy-start.2
  24.0 0.1 reshape.92.state_ref
  24.1 0.6 copy-done.8
  24.7 0.1 copy.29.holder_ref
  24.8 0.0 copy-done
  24.8 0.0 copy-done.1
  24.8 0.0 copy-done.2
  24.9 13.1 %shard_map.149 = (f32[19,64,128]{2,1,0:T(8,128)S(1)}, f32[8,512]{1,0:T(8,128)S(1)}) custom-call(s32[8]{0:T(128)S(1)} %reduce_sum.29.counts_ref, s32[32]{0:T(128)S(1)} %maximum_bitcast_fusion.1.pick_ref, f32[18,512]{1,0:T(8,128)S(1)} %reshape.92.state_ref, f32[128,8,128]{2,1,0:T(8,128)S(1)} %bitcast.18, f32[32,8,128]{2,1,0:T(8,128)S(1)} %bitcast.26, ...), custom_call_target="tpu_custom_call" | custom-call | tf_op jit(solution)/shard_map/pallas_call | solution.py:678
  37.9 21.9 %shard_map.150 = (f32[19,64,128]{2,1,0:T(8,128)S(1)}, f32[18,512]{1,0:T(8,128)S(1)}) custom-call(f32[19,64,128]{2,1,0:T(8,128)S(1)} %get-tuple-element.17.post_ref, s32[64,128]{1,0:T(8,128)S(1)} %bitcast.23, f32[8,512]{1,0:T(8,128)S(1)} %get-tuple-element.18.loads_ref, f32[18,512]{1,0:T(8,128)S(1)} %reshape.92.state_ref), custom_call_target="tpu_custom_call" | custom-call | tf_op jit(solution)/shard_map/pallas_call | solution.py:379
  59.9 12.9 %shard_map.151 = (f32[19,64,128]{2,1,0:T(8,128)S(1)}, f32[8,512]{1,0:T(8,128)S(1)}) custom-call(s32[8]{0:T(128)S(1)} %reduce_sum.29.counts_ref, s32[32]{0:T(128)S(1)} %maximum_bitcast_fusion.1.pick_ref, f32[18,512]{1,0:T(8,128)S(1)} %get-tuple-element.19.state_ref, f32[128,8,128]{2,1,0:T(8,128)S(1)} %bitcast.19, f32[32,8,128]{2,1,0:T(8,128)S(1)} %bitcast.27, ...), custom_call_target="tpu_custom_call" | custom-call | tf_op jit(solution)/shard_map/pallas_call | solution.py:678
  72.8 23.0 %shard_map.152 = (f32[19,64,128]{2,1,0:T(8,128)S(1)}, f32[18,512]{1,0:T(8,128)S(1)}) custom-call(f32[19,64,128]{2,1,0:T(8,128)S(1)} %get-tuple-element.21.post_ref, s32[64,128]{1,0:T(8,128)S(1)} %bitcast.25, f32[8,512]{1,0:T(8,128)S(1)} %get-tuple-element.22.loads_ref, f32[18,512]{1,0:T(8,128)S(1)} %get-tuple-element.19.state_ref), custom_call_target="tpu_custom_call" | custom-call | tf_op jit(solution)/shard_map/pallas_call | solution.py:379
  95.8 0.7 dynamic-slice.1
  96.5 0.7 dynamic-slice
  97.1 0.8 copy.33
  (8 shorter events, 0.1 us)
Async XLA Ops:
  0.6 3.3 %copy-start.6 = (pred[64,64]{1,0:T(32,128)(4,1)S(1)}, pred[64,64]{1,0:T(32,128)(4,1)}, u32[]{:S(2)}) copy-start(pred[64,64]{1,0:T(32,128)(4,1)} %constant.34.clone) | copy-start | bytes 12292
  0.6 6.7 %copy-start.3 = (f32[3,128,64]{1,2,0:T(8,128)S(1)}, f32[3,128,64]{1,2,0:T(8,128)}, u32[]{:S(2)}) copy-start(f32[3,128,64]{1,2,0:T(8,128)} %param.16) | copy-start | bytes 294916
  1.5 4.8 %copy-start.7 = (s32[1,32]{1,0:T(1,128)S(1)}, s32[1,32]{1,0:T(1,128)}, u32[]{:S(2)}) copy-start(s32[1,32]{1,0:T(1,128)} %param.23) | copy-start | bytes 388
  1.5 6.0 %copy-start.5 = (s32[128,64]{0,1:T(8,128)S(1)}, s32[128,64]{0,1:T(8,128)}, u32[]{:S(2)}) copy-start(s32[128,64]{0,1:T(8,128)} %param.21) | copy-start | bytes 98308
  1.5 5.9 %copy-start.4 = (f32[3,128,64]{1,2,0:T(8,128)S(1)}, f32[3,128,64]{1,2,0:T(8,128)}, u32[]{:S(2)}) copy-start(f32[3,128,64]{1,2,0:T(8,128)} %param.20) | copy-start | bytes 294916
  2.4 22.5 %copy-start = (f32[64,16,256]{2,1,0:T(8,128)S(1)}, f32[64,16,256]{2,1,0:T(8,128)}, u32[]{:S(2)}) copy-start(f32[64,16,256]{2,1,0:T(8,128)} %coef_ref.3) | copy-start | bytes 3145732
  7.6 17.2 %copy-start.1 = (f32[19,4,16,128]{3,2,1,0:T(8,128)S(1)}, f32[19,4,16,128]{3,2,1,0:T(8,128)}, u32[]{:S(2)}) copy-start(f32[19,4,16,128]{3,2,1,0:T(8,128)} %param.13) | copy-start | bytes 1867780
  24.0 0.9 copy-start.2
  24.1 0.7 copy-start.8

commit v2 on v1

--- a/solution.py
+++ b/solution.py
@@ -46,10 +46,9 @@
 MESH = pl.DeviceIdType.MESH
 
 
-def rotation_rows(angles):
-    ca, sa = jnp.cos(angles[0]), jnp.sin(angles[0])
-    cb, sb = jnp.cos(angles[1]), jnp.sin(angles[1])
-    cc, sc = jnp.cos(angles[2]), jnp.sin(angles[2])
+def rotation_rows(cosine, sine):
+    ca, cb, cc = cosine
+    sa, sb, sc = sine
     return [
         cc * cb,
         cc * sb * sa - sc * ca,
@@ -130,78 +129,117 @@
     return copy
 
 
+def plan_kernel(
+    route_ref,
+    send_ref,
+    tiles_ref,
+    angles_ref,
+    centers_ref,
+    velocity_ref,
+    slots_ref,
+    contacts_ref,
+    small_ref,
+    count_ref,
+):
+    grains = tiles_ref.shape[0]
+    row = lax.broadcasted_iota(jnp.int32, tiles_ref.shape[1:], 0)
+    slots_ref[...] = jnp.full(slots_ref.shape, -1.0, f32)
+    for owner in range(slots_ref.shape[0]):
+        count_ref[owner] = 0
+
+    def put(grain, carry):
+        owner = route_ref[grain]
+        rank = count_ref[owner]
+        count_ref[owner] = rank + 1
+        slots_ref[owner, rank] = jnp.where(row == 7, grain.astype(f32), tiles_ref[grain])
+        return carry
+
+    lax.fori_loop(0, grains, put, 0, unroll=8)
+
+    def touch(slot, carry):
+        grain = send_ref[slot]
+        contacts_ref[slot] = jnp.where(row == 7, grain.astype(f32), tiles_ref[jnp.maximum(grain, 0)])
+        return carry
+
+    lax.fori_loop(0, contacts_ref.shape[0], touch, 0, unroll=8)
+    angles = angles_ref[...]
+    cosine, sine = jnp.cos(angles), jnp.sin(angles)
+    small_ref[...] = jnp.zeros_like(small_ref)
+    rows = rotation_rows([cosine[i : i + 1] for i in range(3)], [sine[i : i + 1] for i in range(3)])
+    for i, values in enumerate(rows):
+        small_ref[i : i + 1, 0:grains] = values
+    small_ref[9:12, 0:grains] = centers_ref[...]
+    small_ref[12:18, 0:grains] = velocity_ref[...]
+
+
+def plan(owners, cap, route, send, tiles, angles, centers, velocity):
+    grains, _, nodes = tiles.shape
+    vmem = pl.BlockSpec(memory_space=pltpu.VMEM)
+    smem = pl.BlockSpec(memory_space=pltpu.SMEM)
+    return pl.pallas_call(
+        plan_kernel,
+        out_shape=(
+            jax.ShapeDtypeStruct((owners, cap, 8, nodes), f32),
+            jax.ShapeDtypeStruct((send.shape[0], 8, nodes), f32),
+            jax.ShapeDtypeStruct((24, -(-grains // 128) * 128), f32),
+        ),
+        in_specs=[smem, smem] + [vmem] * 4,
+        out_specs=(vmem, vmem, vmem),
+        scratch_shapes=[pltpu.SMEM((owners,), jnp.int32)],
+        compiler_params=pltpu.CompilerParams(vmem_limit_bytes=40 * 1024 * 1024),
+    )(route, send, tiles, angles, centers, velocity)
+
+
 def deal_kernel(
     owners,
-    index_ref,
-    name_ref,
-    tiles_ref,
+    out_slots,
+    out_contacts,
     small_ref,
     slots_ref,
     contacts_ref,
     all_ref,
-    out_slots,
-    out_contacts,
     send_sem,
     recv_sem,
 ):
-    cap, contact_cap = slots_ref.shape[1], contacts_ref.shape[1]
-    width = cap + contact_cap
-    row = lax.broadcasted_iota(jnp.int32, tiles_ref.shape[1:], 0)
     me = owner_index()
-
-    def fill(k, owner, slots, contacts):
-        for r in range(width):
-            at = owner * width + r
-            tile = jnp.where(row == 7, name_ref[at], tiles_ref[index_ref[at]])
-            if r < cap:
-                slots[k, r] = tile
-            else:
-                contacts[k, r - cap] = tile
-
     greet([owner_place(k)[1] for k in range(1, owners)])
     copies = []
     for k in range(1, owners):
         owner, device = owner_place(k)
-        fill(k, owner, out_slots, out_contacts)
         pairs = (
-            (out_slots.at[k], slots_ref.at[me]),
-            (out_contacts.at[k], contacts_ref.at[me]),
+            (out_contacts.at[owner], contacts_ref.at[me]),
             (small_ref, all_ref.at[me]),
+            (out_slots.at[owner], slots_ref.at[me]),
         )
         for i, (source, target) in enumerate(pairs):
             copies.append(remote(source, target, send_sem.at[i, k], recv_sem.at[i, k], device))
-    fill(me, me, slots_ref, contacts_ref)
+    slots_ref[me] = out_slots[me]
+    contacts_ref[me] = out_contacts[me]
     all_ref[me] = small_ref[...]
     for copy in copies:
         copy.wait()
 
 
-def deal(owners, cap, index, name, tiles, small):
-    nodes = tiles.shape[2]
-    contact_cap = index.shape[0] // owners - cap
+def deal(slots, contacts, small):
+    owners = slots.shape[0]
     vmem = pl.BlockSpec(memory_space=pltpu.VMEM)
-    smem = pl.BlockSpec(memory_space=pltpu.SMEM)
-    slots = (owners, cap, 8, nodes)
-    contacts = (owners, contact_cap, 8, nodes)
     return pl.pallas_call(
         functools.partial(deal_kernel, owners),
         out_shape=(
-            jax.ShapeDtypeStruct(slots, f32),
-            jax.ShapeDtypeStruct(contacts, f32),
+            jax.ShapeDtypeStruct(slots.shape, f32),
+            jax.ShapeDtypeStruct(contacts.shape, f32),
             jax.ShapeDtypeStruct((owners,) + small.shape, f32),
         ),
-        in_specs=[smem, smem, vmem, vmem],
+        in_specs=[vmem, vmem, vmem],
         out_specs=(vmem, vmem, vmem),
         scratch_shapes=[
-            pltpu.VMEM(slots, f32),
-            pltpu.VMEM(contacts, f32),
             pltpu.SemaphoreType.DMA((3, owners)),
             pltpu.SemaphoreType.DMA((3, owners)),
         ],
         compiler_params=pltpu.CompilerParams(
             collective_id=0, has_side_effects=True, vmem_limit_bytes=40 * 1024 * 1024
         ),
-    )(index, name, tiles, small)
+    )(slots, contacts, small)
 
 
 def moving(axis, way):
@@ -427,8 +465,9 @@
 def step_kernel(
     size_y,
     tile_cap,
+    owned,
     chunk,
-    counts_ref,
+    group,
     pick_ref,
     state_ref,
     slots_ref,
@@ -459,6 +498,12 @@
         lane = lax.broadcasted_iota(jnp.int32, (ids.shape[0], grains), 1).astype(f32)
         return jnp.where(lane == ids, 1.0, 0.0)
 
+    def named(tiles_ref, per_source):
+        ids = tiles_ref[:, 7, :][:, 0:1]
+        source = lax.broadcasted_iota(jnp.int32, ids.shape, 0).astype(f32)
+        source = jnp.floor((source + 0.5) * (1.0 / per_source))
+        return jnp.where(ids >= 0.0, ids + source * owned, -1.0)
+
     def picked(hot):
         found = lax.dot_general(
             hot, state, (((1,), (1,)), ((), ())), precision=highest, preferred_element_type=f32
@@ -470,7 +515,7 @@
             lane_pack(values), hot, (((0,), (0,)), ((), ())), precision=highest, preferred_element_type=f32
         )[0:8]
 
-    partner_hot = one_hot(contacts_ref[:, 7, :][:, 0:1])
+    partner_hot = one_hot(named(contacts_ref, contact_slots // (tile_slots // tile_cap)))
     holder_hot = one_hot(holder_ref[...])
     partner = picked(partner_hot)
     holder = picked(holder_hot)
@@ -551,7 +596,7 @@
         grid_ref[rows, size_z : 2 * size_z] = low
         grid_ref[rows, 2 * size_z : 3 * size_z] = high
 
-    slot_hot = one_hot(slots_ref[:, 7, :][:, 0:1])
+    slot_hot = one_hot(named(slots_ref, tile_cap))
     own = picked(slot_hot)
     body = [slots_ref[:, i, :] for i in range(3)]
     arm = [own[3 * i] * body[0] + own[3 * i + 1] * body[1] + own[3 * i + 2] * body[2] for i in range(3)]
@@ -560,73 +605,82 @@
         speed_ref[:, i, :] = own[12 + i] + swirl[i]
     force_ref[...] = jnp.zeros_like(force_ref)
     cell_ref[...] = jnp.zeros_like(cell_ref)
-    depth_row = lax.broadcasted_iota(jnp.int32, (size_z, nodes), 0).astype(f32)
+    kind = bf16 if size_z <= 256 else f32
+    depth_row = lax.broadcasted_iota(jnp.int32, (size_z, nodes), 0).astype(f32).astype(kind)
     y_row = lax.broadcasted_iota(jnp.int32, (size_y, nodes), 0).astype(f32)
 
+    def weights_of(slot):
+        tile = slots_ref[slot]
+        cell = tile[6:7]
+        line = jnp.floor((cell + 0.5) * (1.0 / size_z))
+        base_z = cell - line * size_z
+        base_x = jnp.floor((line + 0.5) * (1.0 / size_y))
+        base_y = line - base_x * size_y
+        upper, lower = tile[5:6], 1.0 - tile[5:6]
+        upper_high, upper_low = split(upper)
+        lower_high, lower_low = split(lower)
+        none = jnp.zeros((size_z, nodes), kind)
+        at_low, at_high = depth_row == base_z.astype(kind), depth_row == (base_z + 1.0).astype(kind)
+
+        def placed(low_value, high_value):
+            far = jnp.where(at_high, high_value.astype(kind), none)
+            return jnp.where(at_low, low_value.astype(kind), far).astype(bf16)
+
+        frac_y = tile[4:5]
+        weight_y = jnp.where(
+            y_row == base_y, 1.0 - frac_y, jnp.where(y_row == base_y + 1.0, frac_y, 0.0)
+        )
+        frac_x = tile[3:4]
+        rows = []
+        for x in range(size_x):
+            weight_x = jnp.where(
+                base_x == float(x), 1.0 - frac_x, jnp.where(base_x == float(x - 1), frac_x, 0.0)
+            )
+            rows.append(weight_x * weight_y)
+        high, low = placed(lower_high, upper_high), placed(lower_low, upper_low)
+        return high, low, jnp.concatenate(rows, axis=0)
+
     def spread(start):
-        highs, lows, plane_weights = [], [], []
-        for k in range(chunk):
-            tile = slots_ref[start + k]
-            cell = tile[6:7]
-            line = jnp.floor((cell + 0.5) * (1.0 / size_z))
-            base_z = cell - line * size_z
-            base_x = jnp.floor((line + 0.5) * (1.0 / size_y))
-            base_y = line - base_x * size_y
-            upper, lower = tile[5:6], 1.0 - tile[5:6]
-            upper_high = upper.astype(bf16).astype(f32)
-            lower_high = lower.astype(bf16).astype(f32)
-            at_low, at_high = depth_row == base_z, depth_row == base_z + 1.0
-            highs.append(
-                jnp.where(at_low, lower_high, jnp.where(at_high, upper_high, 0.0)).astype(bf16)
+        starts = [start + part * group for part in range(chunk // group)]
+        sets = [[weights_of(first + k) for k in range(group)] for first in starts]
+        highs = [jnp.concatenate([w[0] for w in each], axis=1) for each in sets]
+        lows = [jnp.concatenate([w[1] for w in each], axis=1) for each in sets]
+        lines = [
+            jnp.dot(
+                grid_ref[...], jnp.concatenate([high, high, low], axis=0), preferred_element_type=f32
             )
-            lows.append(
-                jnp.where(
-                    at_low, lower - lower_high, jnp.where(at_high, upper - upper_high, 0.0)
-                ).astype(bf16)
+            for high, low in zip(highs, lows)
+        ]
+        added = None
+        contract = (((1,), (1,)), ((), ()))
+        for first, each, high, low, line in zip(starts, sets, highs, lows, lines):
+            spread_high, spread_low = [], []
+            for k in range(group):
+                weights = each[k][2]
+                live = jnp.where(slots_ref[first + k][7:8] >= 0.0, ib_stiffness, 0.0)
+                speed = speed_ref[first + k]
+                pieces = []
+                for i in range(3):
+                    taken = line[i * plane : (i + 1) * plane, k * nodes : (k + 1) * nodes]
+                    interp = jnp.sum(taken * weights, axis=0, keepdims=True)
+                    node = live * (speed[i : i + 1] - interp)
+                    force_ref[first + k, i : i + 1, :] = node
+                    pieces.append(node * weights)
+                piece_high, piece_low = split(jnp.concatenate(pieces, axis=0))
+                spread_high.append(piece_high)
+                spread_low.append(piece_low)
+            wide = lax.dot_general(
+                jnp.concatenate(spread_high, axis=1),
+                jnp.concatenate([high, low], axis=0),
+                contract,
+                preferred_element_type=f32,
             )
-            frac_y = tile[4:5]
-            weight_y = jnp.where(
-                y_row == base_y, 1.0 - frac_y, jnp.where(y_row == base_y + 1.0, frac_y, 0.0)
+            narrow = lax.dot_general(
+                jnp.concatenate(spread_low, axis=1), high, contract, preferred_element_type=f32
             )
-            frac_x = tile[3:4]
-            rows = []
-            for x in range(size_x):
-                weight_x = jnp.where(
-                    base_x == float(x), 1.0 - frac_x, jnp.where(base_x == float(x - 1), frac_x, 0.0)
-                )
-                rows.append(weight_x * weight_y)
-            plane_weights.append(jnp.concatenate(rows, axis=0))
-        high = jnp.concatenate(highs, axis=1)
-        low = jnp.concatenate(lows, axis=1)
-        lines = jnp.dot(
-            grid_ref[...], jnp.concatenate([high, high, low], axis=0), preferred_element_type=f32
-        )
-        spread_high, spread_low = [], []
-        for k in range(chunk):
-            weights = plane_weights[k]
-            live = jnp.where(slots_ref[start + k][7:8] >= 0.0, ib_stiffness, 0.0)
-            speed = speed_ref[start + k]
-            pieces, forces = [], []
-            for i in range(3):
-                taken = lines[i * plane : (i + 1) * plane, k * nodes : (k + 1) * nodes]
-                interp = jnp.sum(taken * weights, axis=0, keepdims=True)
-                node = live * (speed[i : i + 1] - interp)
-                force_ref[start + k, i : i + 1, :] = node
-                pieces.append(node * weights)
-            piece_high, piece_low = split(jnp.concatenate(pieces, axis=0))
-            spread_high.append(piece_high)
-            spread_low.append(piece_low)
-        contract = (((1,), (1,)), ((), ()))
-        wide = lax.dot_general(
-            jnp.concatenate(spread_high, axis=1),
-            jnp.concatenate([high, low], axis=0),
-            contract,
-            preferred_element_type=f32,
-        )
-        narrow = lax.dot_general(
-            jnp.concatenate(spread_low, axis=1), high, contract, preferred_element_type=f32
-        )
-        cell_ref[...] += wide[:, 0:size_z] + wide[:, size_z : 2 * size_z] + narrow
+            term = wide[:, 0:size_z] + wide[:, size_z : 2 * size_z] + narrow
+            added = term if added is None else added + term
+        cell_ref[...] += added
 
     for source in range(tile_slots // tile_cap):
 
@@ -634,7 +688,9 @@
             spread(source * tile_cap + turn * chunk)
             return carry
 
-        lax.fori_loop(0, (counts_ref[source] + chunk - 1) // chunk, body_of, 0)
+        ids = slots_ref[source * tile_cap : (source + 1) * tile_cap, 7, :][:, 0:1]
+        count = jnp.sum(jnp.where(ids >= 0.0, 1.0, 0.0)).astype(jnp.int32)
+        lax.fori_loop(0, lax.div(count + (chunk - 1), chunk), body_of, 0)
 
     node = [force_ref[:, i, :] for i in range(3)]
     back = [-total(node[i]) for i in range(3)] + [-total(t) for t in cross(arm, node)]
@@ -667,7 +723,7 @@
             post_ref[q, rows] = jnp.where(wall, flat, relaxed)
 
 
-def run_step(size_y, tile_cap, counts, pick, state, slots, contacts, holder, coefs, fluid, solid):
+def run_step(size_y, tile_cap, owned, pick, state, slots, contacts, holder, coefs, fluid, solid):
     grains = state.shape[1]
     tile_slots, _, nodes = slots.shape
     contact_slots = contacts.shape[0]
@@ -676,12 +732,14 @@
     vmem = pl.BlockSpec(memory_space=pltpu.VMEM)
     smem = pl.BlockSpec(memory_space=pltpu.SMEM)
     return pl.pallas_call(
-        functools.partial(step_kernel, size_y, tile_cap, math.gcd(tile_cap, 4)),
+        functools.partial(
+            step_kernel, size_y, tile_cap, owned, math.gcd(tile_cap, 8), math.gcd(tile_cap, 4)
+        ),
         out_shape=(
             jax.ShapeDtypeStruct(fluid.shape, f32),
             jax.ShapeDtypeStruct((8, grains), f32),
         ),
-        in_specs=[smem, smem] + [vmem] * 7,
+        in_specs=[smem] + [vmem] * 7,
         out_specs=(vmem, vmem),
         scratch_shapes=[
             pltpu.VMEM((6, contact_slots, order, nodes), f32),
@@ -693,7 +751,7 @@
             pltpu.VMEM((3, plane, size_z), f32),
         ],
         compiler_params=pltpu.CompilerParams(vmem_limit_bytes=40 * 1024 * 1024),
-    )(counts, pick, state, slots, contacts, holder, coefs, fluid, solid)
+    )(pick, state, slots, contacts, holder, coefs, fluid, solid)
 
 
 def per_device(
@@ -723,29 +781,16 @@
     me = lax.axis_index("gx") * count_z + lax.axis_index("gz")
     first = (me * grains).astype(f32)
 
-    route = grain_tile[0, :, 0]
-    hot = (route[:, None] == jnp.arange(owners, dtype=jnp.int32)[None, :]).astype(jnp.int32)
-    below = np.tril(np.ones((grains, grains), np.int32), -1)
-    earlier = (route[:, None] == route[None, :]) & (below > 0)
-    rank = jnp.sum(earlier.astype(jnp.int32), axis=1)
-    slot_of = route * tile_cap + rank
-    match = slot_of[:, None] == jnp.arange(tile_slots, dtype=jnp.int32)[None, :]
-    grain_ids = jnp.arange(grains, dtype=jnp.int32)
-    slot_grain = jnp.sum(jnp.where(match, grain_ids[:, None] + 1, 0), axis=0) - 1
-    chosen = jnp.concatenate(
-        [slot_grain.reshape(owners, tile_cap), send_grain[0].reshape(owners, contact_cap)], axis=1
-    ).reshape(-1)
-    name = jnp.where(chosen >= 0, chosen.astype(f32) + first, -1.0)
     tiles = jnp.concatenate(
         [body_nodes, node_frac, node_cell.astype(f32)[None], jnp.zeros((1, nodes, grains), f32)]
     ).transpose(2, 0, 1)
-    rows = rotation_rows(angles) + [centers[i] for i in range(3)] + [velocity[i] for i in range(6)]
-    small = jnp.pad(jnp.stack(rows), ((0, 6), (0, -grains % 128)))
-    slots, contacts, everyone = deal(owners, tile_cap, jnp.maximum(chosen, 0), name, tiles, small)
+    slots, contacts, small = plan(
+        owners, tile_cap, grain_tile[0, :, 0], send_grain[0], tiles, angles, centers, velocity
+    )
+    slots, contacts, everyone = deal(slots, contacts.reshape(owners, contact_cap, 8, nodes), small)
     slots = slots.reshape(tile_slots, 8, nodes)
     contacts = contacts.reshape(contact_slots, 8, nodes)
     state = everyone[:, :18, :grains].transpose(1, 0, 2).reshape(18, owners * grains)
-    counts = jnp.sum((slots[:, 7, 0].reshape(owners, tile_cap) >= 0.0).astype(jnp.int32), axis=1)
     recv = recv_partner[0]
     pick = jnp.maximum(recv, 0)
     holder = jnp.where(recv >= 0, recv.astype(f32) + first, -1.0)[:, None]
@@ -756,7 +801,7 @@
         post, loads = run_step(
             size_y,
             tile_cap,
-            counts,
+            grains,
             pick,
             state,
             slots,

time: 98.1 us -> 79.7 us (0.81)
  Pallas kernels: 84.6 us -> 73.2 us
  other arithmetic: 6.74 us -> 0.11 us
  local copies, waits for them, and re-layouts: 5.77 us -> 4.78 us
    pallas_call x2, Pallas kernels: 44.9 us -> 23.5 us  [exchange(): pl.pallas_call(functools.partial(exchange_kernel, owners, count_y, size_y...]
    pallas_call x2 -> x3, Pallas kernels: 26 us -> 36.7 us  [the longest x2 35.7 us: run_step(): pl.pallas_call(functools.partial(step_kernel, size_y, tile_cap, owned, ma...]
    convert_element_type x1 -> x0, other arithmetic: 2.35 us -> none  [per_device(): (slots[:, 7, 0].reshape(owners, tile_cap) >= 0.0).astype(jnp.int32)]
    mul x2 -> x0, other arithmetic: 1.66 us -> none  [the longest x1 0.85 us: rotation_rows(): cb * ca]
    another operation x2 -> x0, local copies, waits for them, and re-layouts: 1.66 us -> none  [the longest x1 1.58 us: per_device(): small = jnp.pad(jnp.stack(rows), ((0, 6), (0, -grains % 128)))]
    reduce_sum x3 -> x0, other arithmetic: 1.13 us -> none  [the longest x1 0.91 us: per_device(): rank = jnp.sum(earlier.astype(jnp.int32), axis=1)]
    unnamed x22 -> x25, local copies, waits for them, and re-layouts: 2.18 us -> 3.19 us
where the time goes in v2:
time: 79.7 us; the launch traced here: 79 us
  Pallas kernels  73.2 us (92%)
  local copies, waits for them, and re-layouts  4.78 us (6%)
  between operations  0.85 us (1%)
    pallas_call x2, Pallas kernels, run_step(): pl.pallas_call(functools.partial(step_kernel, size_y, tile_cap, owned, ma...  35.7 us
    pallas_call x2, Pallas kernels, exchange(): pl.pallas_call(functools.partial(exchange_kernel, owners, count_y, size_y...  23.5 us
    pallas_call x1, Pallas kernels, deal(): pl.pallas_call(functools.partial(deal_kernel, owners), out_shape=(jax.Sha...  13 us
    unnamed x25, local copies, waits for them, and re-layouts  3.19 us

profile of v2, /device:TPU:0, one launch (start us, length us, event | category | flops | bytes accessed | tf_op | source)
XLA Modules:
  0.0 79.0 jit_solution(214193032977806047)
XLA Ops:
  0.6 0.0 copy-start.8
  0.6 1.0 %copy.15 = f32[3,128,64]{1,0,2:T(4,128)S(1)} copy(f32[3,128,64]{1,2,0:T(8,128)} %param.15) | data formatting | bytes 196608 | tf_op args[3]
  1.6 0.0 copy-done.8
  1.6 0.0 copy-start.9
  1.7 0.0 copy-start.3
  1.7 0.0 copy-start.4
  1.7 0.0 copy-start.5
  1.7 0.0 copy-start.6
  1.7 0.0 copy-start.7
  1.7 0.1 copy.16
  1.8 0.6 copy-done.9
  2.4 0.0 copy-start
  2.4 0.1 pad.3.clone
  2.5 0.1 maximum_bitcast_fusion.tiles_ref
  2.6 0.0 copy-done.3
  2.6 0.0 copy-done.4
  2.6 0.0 copy-done.5
  2.6 0.0 copy-done.6
  2.6 0.0 copy-done.7
  2.6 1.0 %shard_map.139 = (f32[8,16,8,128]{3,2,1,0:T(8,128)S(1)}, f32[32,8,128]{2,1,0:T(8,128)S(1)}, f32[24,128]{1,0:T(8,128)S(1)}) custom-call(s32[64]{0:T(128)S(1)} %bitcast.29, s32[32]{0:T(128)S(1)} %bitcast.30, f32[64,8,128]{2,1,0:T(8,128)S(1)} %maximum_bitcast_fusion.tiles_ref, f32[3,64]{1,0:T(4,128)S(1)} %copy-done.4, f32[3,64]{1,0:T(4,128)S(1)} %copy-done.5, ...), custom_call_target="tpu_custom_call" | custom-call | tf_op jit(solution)/shard_map/pallas_call | solution.py:179
  3.7 0.0 copy-start.1
  3.7 13.0 %shard_map.140 = (f32[8,16,8,128]{3,2,1,0:T(8,128)S(1)}, f32[8,4,8,128]{3,2,1,0:T(8,128)S(1)}, f32[8,24,128]{2,1,0:T(8,128)S(1)}) custom-call(f32[8,16,8,128]{3,2,1,0:T(8,128)S(1)} %get-tuple-element.17.out_slots, f32[8,4,8,128]{3,2,1,0:T(8,128)S(1)} %bitcast.28, f32[24,128]{1,0:T(8,128)S(1)} %get-tuple-element.19.small_ref), custom_call_target="tpu_custom_call" | custom-call | tf_op jit(solution)/shard_map/pallas_call | solution.py:226
  16.8 0.0 copy-start.10
  16.8 0.1 reshape.62.state_ref
  16.8 0.0 copy-start.2
  16.9 0.6 copy-done.10
  17.4 0.1 copy.18.holder_ref
  17.5 0.0 copy-done
  17.5 0.0 copy-done.1
  17.5 0.1 copy-done.2
  17.6 18.0 %shard_map.141 = (f32[19,64,128]{2,1,0:T(8,128)S(1)}, f32[8,512]{1,0:T(8,128)S(1)}) custom-call(s32[32]{0:T(128)S(1)} %maximum_bitcast_fusion.1.pick_ref, f32[18,512]{1,0:T(8,128)S(1)} %reshape.62.state_ref, f32[128,8,128]{2,1,0:T(8,128)S(1)} %bitcast.18, f32[32,8,128]{2,1,0:T(8,128)S(1)} %bitcast.26, f32[32,1]{1,0:T(8,128)S(1)} %copy.18.holder_ref, ...), custom_call_target="tpu_custom_call" | custom-call | tf_op jit(solution)/shard_map/pallas_call | solution.py:734
  35.6 11.8 %shard_map.142 = (f32[19,64,128]{2,1,0:T(8,128)S(1)}, f32[18,512]{1,0:T(8,128)S(1)}) custom-call(f32[19,64,128]{2,1,0:T(8,128)S(1)} %get-tuple-element.23.post_ref, s32[64,128]{1,0:T(8,128)S(1)} %bitcast.23, f32[8,512]{1,0:T(8,128)S(1)} %get-tuple-element.24.loads_ref, f32[18,512]{1,0:T(8,128)S(1)} %reshape.62.state_ref), custom_call_target="tpu_custom_call" | custom-call | tf_op jit(solution)/shard_map/pallas_call | solution.py:417
  47.3 17.8 %shard_map.143 = (f32[19,64,128]{2,1,0:T(8,128)S(1)}, f32[8,512]{1,0:T(8,128)S(1)}) custom-call(s32[32]{0:T(128)S(1)} %maximum_bitcast_fusion.1.pick_ref, f32[18,512]{1,0:T(8,128)S(1)} %get-tuple-element.25.state_ref, f32[128,8,128]{2,1,0:T(8,128)S(1)} %bitcast.19, f32[32,8,128]{2,1,0:T(8,128)S(1)} %bitcast.27, f32[32,1]{1,0:T(8,128)S(1)} %copy.18.holder_ref, ...), custom_call_target="tpu_custom_call" | custom-call | tf_op jit(solution)/shard_map/pallas_call | solution.py:734
  65.1 11.7 %shard_map.144 = (f32[19,64,128]{2,1,0:T(8,128)S(1)}, f32[18,512]{1,0:T(8,128)S(1)}) custom-call(f32[19,64,128]{2,1,0:T(8,128)S(1)} %get-tuple-element.27.post_ref, s32[64,128]{1,0:T(8,128)S(1)} %bitcast.25, f32[8,512]{1,0:T(8,128)S(1)} %get-tuple-element.28.loads_ref, f32[18,512]{1,0:T(8,128)S(1)} %get-tuple-element.25.state_ref), custom_call_target="tpu_custom_call" | custom-call | tf_op jit(solution)/shard_map/pallas_call | solution.py:417
  76.8 0.7 dynamic-slice.1
  77.5 0.7 dynamic-slice
  78.2 0.8 %copy.21 = f32[19,4,16,128]{3,2,1,0:T(8,128)} copy(f32[19,4,16,128]{3,2,1,0:T(8,128)S(1)} %bitcast.21) | data formatting | bytes 1245184
  (5 shorter events, 0.0 us)
Async XLA Ops:
  0.6 1.0 %copy-start.8 = (f32[3,128,64]{1,2,0:T(8,128)S(1)}, f32[3,128,64]{1,2,0:T(8,128)}, u32[]{:S(2)}) copy-start(f32[3,128,64]{1,2,0:T(8,128)} %param.19) | copy-start | bytes 294916
  1.6 0.8 copy-start.9
  1.7 0.9 %copy-start.3 = (f32[6,64]{1,0:T(8,128)S(1)}, f32[6,64]{1,0:T(8,128)}, u32[]{:S(2)}) copy-start(f32[6,64]{1,0:T(8,128)} %velocity_ref.1) | copy-start | bytes 4612
  1.7 0.9 %copy-start.4 = (f32[3,64]{1,0:T(4,128)S(1)}, f32[3,64]{1,0:T(4,128)}, u32[]{:S(2)}) copy-start(f32[3,64]{1,0:T(4,128)} %angles_ref.1) | copy-start | bytes 2308
  1.7 0.9 %copy-start.5 = (f32[3,64]{1,0:T(4,128)S(1)}, f32[3,64]{1,0:T(4,128)}, u32[]{:S(2)}) copy-start(f32[3,64]{1,0:T(4,128)} %centers_ref.1) | copy-start | bytes 2308
  1.7 0.9 %copy-start.6 = (s32[1,64,1]{1,2,0:T(1,128)S(1)}, s32[1,64,1]{1,2,0:T(1,128)}, u32[]{:S(2)}) copy-start(s32[1,64,1]{1,2,0:T(1,128)} %param.21) | copy-start | bytes 772
  1.7 0.9 %copy-start.7 = (s32[1,32]{1,0:T(1,128)S(1)}, s32[1,32]{1,0:T(1,128)}, u32[]{:S(2)}) copy-start(s32[1,32]{1,0:T(1,128)} %param.22) | copy-start | bytes 388
  2.4 15.1 %copy-start = (f32[64,16,256]{2,1,0:T(8,128)S(1)}, f32[64,16,256]{2,1,0:T(8,128)}, u32[]{:S(2)}) copy-start(f32[64,16,256]{2,1,0:T(8,128)} %coef_ref.3) | copy-start | bytes 3145732
  3.7 13.9 %copy-start.1 = (f32[19,4,16,128]{3,2,1,0:T(8,128)S(1)}, f32[19,4,16,128]{3,2,1,0:T(8,128)}, u32[]{:S(2)}) copy-start(f32[19,4,16,128]{3,2,1,0:T(8,128)} %param.12) | copy-start | bytes 1867780
  16.8 0.7 copy-start.10
  16.8 0.8 copy-start.2

commit v3 on v2

--- a/solution.py
+++ b/solution.py
@@ -310,6 +310,18 @@
         z_copies.append(remote(z_out.at[i], z_in.at[i], send_sem.at[i], recv_sem.at[i], place(0, 0, way)))
     for copy in z_copies:
         copy.wait()
+    for copy in owner_copies:
+        copy.wait()
+    added = owner_in[me]
+    for j in range(1, owners):
+        added = added + owner_in[lax.rem(me - j + owners, owners)]
+    owner_sum[...] = added
+    slab_copies = [
+        remote(owner_sum, slab_in.at[k], slab_send.at[k], slab_recv.at[k], place(0, k, 0))
+        for k in range(1, count_y)
+    ]
+    slab_in[0] = added
+
     slot_of = {}
     for i, way in enumerate(ways):
         packed = z_in[i]
@@ -354,20 +366,6 @@
             )
         )
 
-    for copy in owner_copies:
-        copy.wait()
-    added = owner_in[me]
-    for j in range(1, owners):
-        added = added + owner_in[lax.rem(me - j + owners, owners)]
-    owner_sum[...] = added
-    slab_copies = [
-        remote(owner_sum, slab_in.at[k], slab_send.at[k], slab_recv.at[k], place(0, k, 0))
-        for k in range(1, count_y)
-    ]
-    slab_in[0] = added
-
-    for copy in copies:
-        copy.wait()
     y_row = lax.broadcasted_iota(jnp.int32, (size_y, size_z), 0)
 
     def moved(q, x):
@@ -387,14 +385,25 @@
             values = jnp.where(y_row == edge, line, pltpu.roll(values, way_y % size_y, 0))
         return values
 
-    for x in range(size_x):
-        rows = pl.ds(x * size_y, size_y)
-        wall = solid_ref[rows] > 0
-        fluid_ref[0, rows] = moved(0, x)
-        for q in range(1, directions, 2):
-            here, there = moved(q, x), moved(q + 1, x)
-            fluid_ref[q, rows] = jnp.where(wall, there, here)
-            fluid_ref[q + 1, rows] = jnp.where(wall, here, there)
+    def inner(q, x):
+        way_x, way_y = int(lattice_dirs[q][0]), int(lattice_dirs[q][1])
+        return way_y == 0 and (way_x == 0 or 0 < x < size_x - 1)
+
+    for early in (True, False):
+        if not early:
+            for copy in copies:
+                copy.wait()
+        for x in range(size_x):
+            rows = pl.ds(x * size_y, size_y)
+            wall = solid_ref[rows] > 0
+            if early:
+                fluid_ref[0, rows] = moved(0, x)
+            for q in range(1, directions, 2):
+                if inner(q, x) != early:
+                    continue
+                here, there = moved(q, x), moved(q + 1, x)
+                fluid_ref[q, rows] = jnp.where(wall, there, here)
+                fluid_ref[q + 1, rows] = jnp.where(wall, here, there)
 
     for copy in slab_copies:
         copy.wait()
@@ -812,8 +821,8 @@
             solid_flat,
         )
         fluid, state = exchange(owners, lax.axis_size("gy"), size_y, post, solid_flat, loads, state)
-    state = lax.dynamic_slice_in_dim(state, me * grains, grains, axis=1)
-    return (fluid.reshape(populations.shape), state[9:12], state[12:18])
+    state = lax.dynamic_slice(state, (9, me * grains), (9, grains))
+    return (fluid.reshape(populations.shape), state[0:3], state[3:9])
 
 
 def solution(mesh):

time: 79.7 us -> 82.6 us (1.036)
  Pallas kernels: 73.2 us -> 76 us
    pallas_call x2, Pallas kernels: 23.5 us -> 35.4 us  [exchange(): pl.pallas_call(functools.partial(exchange_kernel, owners, count_y, size_y...]
    pallas_call x2, Pallas kernels: 35.7 us -> 26.5 us  [run_step(): pl.pallas_call(functools.partial(step_kernel, size_y, tile_cap, owned, ma...]
where the time goes in v3:
time: 82.6 us; the launch traced here: 81.7 us
  Pallas kernels  76 us (92%)
  local copies, waits for them, and re-layouts  4.78 us (6%)
  between operations  0.85 us (1%)
    pallas_call x2, Pallas kernels, exchange(): pl.pallas_call(functools.partial(exchange_kernel, owners, count_y, size_y...  35.4 us
    pallas_call x2, Pallas kernels, run_step(): pl.pallas_call(functools.partial(step_kernel, size_y, tile_cap, owned, ma...  26.5 us
    pallas_call x1, Pallas kernels, deal(): pl.pallas_call(functools.partial(deal_kernel, owners), out_shape=(jax.Sha...  13 us
    unnamed x25, local copies, waits for them, and re-layouts  3.19 us

profile of v3, /device:TPU:0, one launch (start us, length us, event | category | flops | bytes accessed | tf_op | source)
XLA Modules:
  0.0 81.7 jit_solution(17903324393755748733)
XLA Ops:
  0.6 0.0 copy-start.8
  0.6 1.0 %copy.15 = f32[3,128,64]{1,0,2:T(4,128)S(1)} copy(f32[3,128,64]{1,2,0:T(8,128)} %param.15) | data formatting | bytes 196608 | tf_op args[3]
  1.6 0.0 copy-done.8
  1.6 0.0 copy-start.9
  1.7 0.0 copy-start.3
  1.7 0.0 copy-start.4
  1.7 0.0 copy-start.5
  1.7 0.0 copy-start.6
  1.7 0.0 copy-start.7
  1.7 0.1 copy.16
  1.8 0.6 copy-done.9
  2.4 0.0 copy-start
  2.4 0.1 pad.3.clone
  2.5 0.1 maximum_bitcast_fusion.tiles_ref
  2.6 0.0 copy-done.3
  2.6 0.0 copy-done.4
  2.6 0.0 copy-done.5
  2.6 0.0 copy-done.6
  2.6 0.0 copy-done.7
  2.6 1.0 %shard_map.139 = (f32[8,16,8,128]{3,2,1,0:T(8,128)S(1)}, f32[32,8,128]{2,1,0:T(8,128)S(1)}, f32[24,128]{1,0:T(8,128)S(1)}) custom-call(s32[64]{0:T(128)S(1)} %bitcast.29, s32[32]{0:T(128)S(1)} %bitcast.30, f32[64,8,128]{2,1,0:T(8,128)S(1)} %maximum_bitcast_fusion.tiles_ref, f32[3,64]{1,0:T(4,128)S(1)} %copy-done.4, f32[3,64]{1,0:T(4,128)S(1)} %copy-done.5, ...), custom_call_target="tpu_custom_call" | custom-call | tf_op jit(solution)/shard_map/pallas_call | solution.py:179
  3.7 0.0 copy-start.1
  3.7 13.0 %shard_map.140 = (f32[8,16,8,128]{3,2,1,0:T(8,128)S(1)}, f32[8,4,8,128]{3,2,1,0:T(8,128)S(1)}, f32[8,24,128]{2,1,0:T(8,128)S(1)}) custom-call(f32[8,16,8,128]{3,2,1,0:T(8,128)S(1)} %get-tuple-element.17.out_slots, f32[8,4,8,128]{3,2,1,0:T(8,128)S(1)} %bitcast.28, f32[24,128]{1,0:T(8,128)S(1)} %get-tuple-element.19.small_ref), custom_call_target="tpu_custom_call" | custom-call | tf_op jit(solution)/shard_map/pallas_call | solution.py:226
  16.8 0.0 copy-start.10
  16.8 0.1 reshape.62.state_ref
  16.8 0.0 copy-start.2
  16.9 0.6 copy-done.10
  17.4 0.1 copy.18.holder_ref
  17.5 0.0 copy-done
  17.5 0.0 copy-done.1
  17.5 0.1 copy-done.2
  17.6 13.3 %shard_map.141 = (f32[19,64,128]{2,1,0:T(8,128)S(1)}, f32[8,512]{1,0:T(8,128)S(1)}) custom-call(s32[32]{0:T(128)S(1)} %maximum_bitcast_fusion.1.pick_ref, f32[18,512]{1,0:T(8,128)S(1)} %reshape.62.state_ref, f32[128,8,128]{2,1,0:T(8,128)S(1)} %bitcast.18, f32[32,8,128]{2,1,0:T(8,128)S(1)} %bitcast.26, f32[32,1]{1,0:T(8,128)S(1)} %copy.18.holder_ref, ...), custom_call_target="tpu_custom_call" | custom-call | tf_op jit(solution)/shard_map/pallas_call | solution.py:743
  30.9 18.7 %shard_map.142 = (f32[19,64,128]{2,1,0:T(8,128)S(1)}, f32[18,512]{1,0:T(8,128)S(1)}) custom-call(f32[19,64,128]{2,1,0:T(8,128)S(1)} %get-tuple-element.23.post_ref, s32[64,128]{1,0:T(8,128)S(1)} %bitcast.23, f32[8,512]{1,0:T(8,128)S(1)} %get-tuple-element.24.loads_ref, f32[18,512]{1,0:T(8,128)S(1)} %reshape.62.state_ref), custom_call_target="tpu_custom_call" | custom-call | tf_op jit(solution)/shard_map/pallas_call | solution.py:426
  49.6 13.2 %shard_map.143 = (f32[19,64,128]{2,1,0:T(8,128)S(1)}, f32[8,512]{1,0:T(8,128)S(1)}) custom-call(s32[32]{0:T(128)S(1)} %maximum_bitcast_fusion.1.pick_ref, f32[18,512]{1,0:T(8,128)S(1)} %get-tuple-element.25.state_ref, f32[128,8,128]{2,1,0:T(8,128)S(1)} %bitcast.19, f32[32,8,128]{2,1,0:T(8,128)S(1)} %bitcast.27, f32[32,1]{1,0:T(8,128)S(1)} %copy.18.holder_ref, ...), custom_call_target="tpu_custom_call" | custom-call | tf_op jit(solution)/shard_map/pallas_call | solution.py:743
  62.8 16.8 %shard_map.144 = (f32[19,64,128]{2,1,0:T(8,128)S(1)}, f32[18,512]{1,0:T(8,128)S(1)}) custom-call(f32[19,64,128]{2,1,0:T(8,128)S(1)} %get-tuple-element.27.post_ref, s32[64,128]{1,0:T(8,128)S(1)} %bitcast.25, f32[8,512]{1,0:T(8,128)S(1)} %get-tuple-element.28.loads_ref, f32[18,512]{1,0:T(8,128)S(1)} %get-tuple-element.25.state_ref), custom_call_target="tpu_custom_call" | custom-call | tf_op jit(solution)/shard_map/pallas_call | solution.py:426
  79.6 0.7 dynamic-slice.1
  80.2 0.7 constant_dynamic-slice_fusion
  80.9 0.8 %copy.21 = f32[19,4,16,128]{3,2,1,0:T(8,128)} copy(f32[19,4,16,128]{3,2,1,0:T(8,128)S(1)} %bitcast.21) | data formatting | bytes 1245184
  (5 shorter events, 0.0 us)
Async XLA Ops:
  0.6 1.0 %copy-start.8 = (f32[3,128,64]{1,2,0:T(8,128)S(1)}, f32[3,128,64]{1,2,0:T(8,128)}, u32[]{:S(2)}) copy-start(f32[3,128,64]{1,2,0:T(8,128)} %param.19) | copy-start | bytes 294916
  1.6 0.8 copy-start.9
  1.7 0.9 %copy-start.3 = (f32[6,64]{1,0:T(8,128)S(1)}, f32[6,64]{1,0:T(8,128)}, u32[]{:S(2)}) copy-start(f32[6,64]{1,0:T(8,128)} %velocity_ref.1) | copy-start | bytes 4612
  1.7 0.9 %copy-start.4 = (f32[3,64]{1,0:T(4,128)S(1)}, f32[3,64]{1,0:T(4,128)}, u32[]{:S(2)}) copy-start(f32[3,64]{1,0:T(4,128)} %angles_ref.1) | copy-start | bytes 2308
  1.7 0.9 %copy-start.5 = (f32[3,64]{1,0:T(4,128)S(1)}, f32[3,64]{1,0:T(4,128)}, u32[]{:S(2)}) copy-start(f32[3,64]{1,0:T(4,128)} %centers_ref.1) | copy-start | bytes 2308
  1.7 0.9 %copy-start.6 = (s32[1,64,1]{1,2,0:T(1,128)S(1)}, s32[1,64,1]{1,2,0:T(1,128)}, u32[]{:S(2)}) copy-start(s32[1,64,1]{1,2,0:T(1,128)} %param.21) | copy-start | bytes 772
  1.7 0.9 %copy-start.7 = (s32[1,32]{1,0:T(1,128)S(1)}, s32[1,32]{1,0:T(1,128)}, u32[]{:S(2)}) copy-start(s32[1,32]{1,0:T(1,128)} %param.22) | copy-start | bytes 388
  2.4 15.1 %copy-start = (f32[64,16,256]{2,1,0:T(8,128)S(1)}, f32[64,16,256]{2,1,0:T(8,128)}, u32[]{:S(2)}) copy-start(f32[64,16,256]{2,1,0:T(8,128)} %coef_ref.3) | copy-start | bytes 3145732
  3.7 13.9 %copy-start.1 = (f32[19,4,16,128]{3,2,1,0:T(8,128)S(1)}, f32[19,4,16,128]{3,2,1,0:T(8,128)}, u32[]{:S(2)}) copy-start(f32[19,4,16,128]{3,2,1,0:T(8,128)} %param.12) | copy-start | bytes 1867780
  16.8 0.7 copy-start.10
  16.8 0.8 copy-start.2
